TPU v7x, 128 devices: a whole 4x4x4 slice. The times are simulated.
128 devices in a mesh: px: 8 (over x, core), py: 16 (over z, y).
Axes of the slice: x: 4, y: 4, z: 4, core: 2. Of those that a mesh axis runs over, the one named last changes fastest.
Arguments:
- control_init: float32 [16, 1024, 1024], P(None, ('px', 'py')), may hold values from -3 to 3
- kernel_x: float32 [16, 64], replicated, may hold values from 0 to 0.25
- kernel_y: float32 [16, 64], replicated, may hold values from 0 to 0.25
- obs_weight: float32 [431], replicated, may hold values from 0.3 to 3
- jacobian: bfloat16 [16384, 16, 431], P(('px', 'py')), may hold values from -0.3125 to 0.3125
- innovation: bfloat16 [16384, 431], P(('px', 'py')), may hold values from -24 to 24
- obs_dest: int32 [16384, 1], P(('px', 'py')), may hold values from 0 to 127; in each aligned block of 128 rows (0 to 127, 128 to 255, ...) at most 2 rows name the same one
- obs_cell: int32 [16384], P(('px', 'py')), may hold values from 0 to 8191
Outputs:
- control: float32 [16, 1024, 1024], P(None, ('px', 'py'))
- residual: float32 [16, 1024, 1024], P(None, ('px', 'py'))
Inputs may be any that keep to these rules, and one draw needn't show every extreme that they name: `obs_dest`: within the 128 rows of one device, no owner is named by more than 2 rows; some owner is named by exactly 2. `obs_cell`: column within the owner's block of 8 grid columns by 1024 rows, numbered local column * 1024 + row.
All inputs are finite; a program needn't handle non-finite values.
Results may differ from a plain program's by a relative error of at most 0.003.
Values may be sent and summed in bfloat16 or wider, within the bound.
A program may use at most 128 MiB of HBM per device.

v0:
```python
import jax
import jax.numpy as jnp
from jax import lax
from jax.sharding import PartitionSpec as P

ITERS = 2


def band_table(kernel, flipped):
    tap_count = kernel.shape[1]
    window_len = 128 + tap_count
    row_index = jnp.arange(window_len, dtype=jnp.int32)[:, None, None]
    col_index = jnp.arange(128, dtype=jnp.int32)[None, :, None]
    tap_index = jnp.arange(tap_count, dtype=jnp.int32)[None, None, :]
    target = tap_count - tap_index if flipped else tap_index
    matches = (row_index - col_index == target).astype(jnp.float32)
    return jnp.einsum("jit,lt->lji", matches, kernel, precision=lax.Precision.HIGHEST)


def convolve(grid_field, banded, periodic, transposed):
    levels, row_count, length = grid_field.shape
    block_count = length // 128
    half_span = (banded.shape[1] - 128) // 2
    blocks = grid_field.reshape(levels, row_count, block_count, 128)
    before = jnp.roll(blocks, 1, axis=2)[..., 128 - half_span :]
    following = jnp.roll(blocks, -1, axis=2)[..., :half_span]
    if not periodic:
        block_index = jnp.arange(block_count, dtype=jnp.int32)
        before = before * (block_index > 0).astype(jnp.float32)[:, None]
        following = following * (block_index < block_count - 1).astype(jnp.float32)[:, None]
    window = jnp.concatenate([before, blocks, following], axis=3)
    if transposed:
        result = jnp.einsum("lrbj,lji->lbir", window, banded, precision=lax.Precision.HIGHEST)
        return result.reshape(levels, length, row_count)
    result = jnp.einsum("lrbj,lji->lrbi", window, banded, precision=lax.Precision.HIGHEST)
    return result.reshape(levels, row_count, length)


def per_device(
    control_init, kernel_x, kernel_y, obs_weight, jacobian, innovation, obs_dest, obs_cell
):
    forward_x = band_table(kernel_x, False)
    forward_y = band_table(kernel_y, False)
    backward_x = band_table(kernel_x, True)
    backward_y = band_table(kernel_y, True)
    levels = control_init.shape[0]
    devices = lax.axis_size(("px", "py"))
    obs_count = obs_dest.shape[0]
    capacity = max(2, 2 * obs_count // devices)
    slot_total = devices * capacity
    target = obs_dest[:, 0]
    one_hot = (target[:, None] == jnp.arange(devices, dtype=jnp.int32)[None, :]).astype(jnp.int32)
    earlier = jnp.cumsum(one_hot, axis=0) - one_hot
    position = target * capacity + jnp.sum(earlier * one_hot, axis=1)
    cell_slots = jnp.zeros((slot_total,), jnp.int32).at[position].set(obs_cell)

    def to_columns(row_major):
        return lax.all_to_all(row_major, ("px", "py"), split_axis=1, concat_axis=2, tiled=True)

    def to_rows(column_major):
        return lax.all_to_all(column_major, ("px", "py"), split_axis=1, concat_axis=2, tiled=True)

    def spread(values):
        return convolve(
            to_columns(convolve(values, forward_x, True, True)), forward_y, False, False
        )

    def gather_back(values):
        return convolve(to_rows(convolve(values, backward_y, False, True)), backward_x, True, False)

    def respond(profile, local_jac, local_innov, use_innovation):
        evolved = jnp.einsum("olc,ol->oc", local_jac, profile, preferred_element_type=jnp.float32)
        if use_innovation:
            evolved = evolved - local_innov.astype(jnp.float32)
        weighted = (obs_weight[None, :] * evolved).astype(jnp.bfloat16)
        return jnp.einsum("olc,oc->ol", local_jac, weighted, preferred_element_type=jnp.float32)

    jac_pack = (
        jnp.zeros((slot_total,) + jacobian.shape[1:], jnp.bfloat16).at[position].set(jacobian)
    )
    innov_pack = (
        jnp.zeros((slot_total,) + innovation.shape[1:], jnp.bfloat16).at[position].set(innovation)
    )
    jac_slots, innov_slots, owned_cells = (
        lax.all_to_all(jac_pack, ("px", "py"), split_axis=0, concat_axis=0, tiled=True),
        lax.all_to_all(innov_pack, ("px", "py"), split_axis=0, concat_axis=0, tiled=True),
        lax.all_to_all(cell_slots, ("px", "py"), split_axis=0, concat_axis=0, tiled=True),
    )

    def observe(increment, use_innovation):
        flat_field = increment.reshape(levels, -1)
        profile = flat_field[:, owned_cells].T.astype(jnp.bfloat16)
        adjoint_rows = respond(profile, jac_slots, innov_slots, use_innovation)
        result = jnp.zeros_like(flat_field).at[:, owned_cells].add(adjoint_rows.T)
        return result.reshape(increment.shape)

    def inner(first, second):
        return lax.psum(jnp.sum(first * second), ("px", "py"))

    gradient = control_init + gather_back(observe(spread(control_init), True))
    residual = -gradient
    direction = residual
    control = control_init
    norm_now = inner(residual, residual)
    for iteration in range(ITERS):
        image = direction + gather_back(observe(spread(direction), False))
        alpha = norm_now / inner(direction, image)
        control = control + alpha * direction
        residual = residual - alpha * image
        norm_next = inner(residual, residual)
        direction = residual + norm_next / norm_now * direction
        norm_now = norm_next
    return (control, residual)


def solution(mesh):
    in_specs = (
        P(None, ("px", "py"), None),
        P(),
        P(),
        P(),
        P(("px", "py"), None, None),
        P(("px", "py"), None),
        P(("px", "py"), None),
        P(("px", "py")),
    )
    out_specs = (P(None, ("px", "py"), None), P(None, ("px", "py"), None))
    return jax.shard_map(
        per_device, mesh=mesh, in_specs=in_specs, out_specs=out_specs, check_vma=False
    )
```

profile of v0, /device:TPU:1, one launch (start us, length us, event | category | flops | bytes accessed | tf_op | source)
XLA Modules:
  0.0 657.8 jit_solution(2112721562370766012)
XLA Ops:
  5.0 11.5 %all-to-all-start = ((s32[128,2,1]{1,2,0:T(1,128)}), s32[128,2,1]{1,2,0:T(1,128)S(1)}, u32[]{:S(2)}, u32[]{:S(2)}) async-start(s32[128,2,1]{1,2,0:T(1,128)} %bitcast.6), calls=%async_computation | async-start | bytes 131072 | tf_op jit(solution)/shard_map/all_to_all | solution.py:87
  26.2 6.9 %all-to-all-start.3 = ((bf16[128,2,431]{2,1,0:T(2,128)(2,1)}), bf16[128,2,431]{2,1,0:T(2,128)(2,1)S(1)}, u32[]{:S(2)}, u32[]{:S(2)}) async-start(bf16[128,2,431]{2,1,0:T(2,128)(2,1)} %all_to_all.90), calls=%async_computation.3 | async-start | bytes 524288 | tf_op jit(solution)/shard_map/all_to_all | solution.py:86
  39.9 4.2 reshape.266
  44.6 9.3 %all-to-all-start.2 = ((f32[128,1,1024]{2,1,0:T(1,128)}), f32[128,1,1024]{2,1,0:T(1,128)S(1)}, u32[]{:S(2)}, u32[]{:S(2)}) async-start(f32[128,1,1024]{2,1,0:T(1,128)} %reshape.266), calls=%async_computation.2 | async-start | bytes 1048576 | tf_op jit(solution)/shard_map/all_to_all | solution.py:58
  53.9 4.9 copy.95
  61.3 17.6 %scatter_fusion = bf16[256,16,431]{2,1,0:T(8,128)(2,1)} fusion(bf16[256,16,431]{2,1,0:T(8,128)(2,1)} %broadcast_in_dim.4, s32[128]{0:T(128)S(1)} %fusion.178, bf16[128,16,431]{2,1,0:T(8,128)(2,1)} %copy.95), kind=kCustom, calls=%fused_computation.4 | custom fusion | bytes 5296640 | tf_op jit(solution)/shard_map/scatter | solution.py:79
  79.7 10.3 %all-to-all-start.1 = ((bf16[256,16,431]{2,1,0:T(8,128)(2,1)}), bf16[256,16,431]{2,1,0:T(8,128)(2,1)}, u32[]{:S(2)}, u32[]{:S(2)}) async-start(bf16[256,16,431]{2,1,0:T(8,128)(2,1)} %scatter_fusion), calls=%async_computation.1 | async-start | bytes 8388608 | tf_op jit(solution)/shard_map/all_to_all | solution.py:85
  107.7 4.4 copy.98
  126.0 14.6 %all-to-all-done.1 = bf16[256,16,431]{2,1,0:T(8,128)(2,1)} async-done(((bf16[256,16,431]{2,1,0:T(8,128)(2,1)}), bf16[256,16,431]{2,1,0:T(8,128)(2,1)}, u32[]{:S(2)}, u32[]{:S(2)}) %all-to-all-start.1) | async-done | bytes 3530784 | tf_op jit(solution)/shard_map/all_to_all | solution.py:85
  161.1 4.2 copy.190
  165.2 4.2 reshape.268
  169.4 6.8 %all-to-all-start.4 = ((f32[128,1,1024]{2,1,0:T(1,128)}), f32[128,1,1024]{2,1,0:T(1,128)}, u32[]{:S(2)}, u32[]{:S(2)}) async-start(f32[128,1,1024]{2,1,0:T(1,128)} %reshape.268), calls=%async_computation.4 | async-start | bytes 1048576 | tf_op jit(solution)/shard_map/all_to_all | solution.py:61
  179.3 10.4 %all-to-all-done.4 = f32[128,1,1024]{2,1,0:T(1,128)} async-done(((f32[128,1,1024]{2,1,0:T(1,128)}), f32[128,1,1024]{2,1,0:T(1,128)}, u32[]{:S(2)}, u32[]{:S(2)}) %all-to-all-start.4) | async-done | bytes 524320 | tf_op jit(solution)/shard_map/all_to_all | solution.py:61
  197.1 4.4 copy.110
  218.8 4.2 copy.197
  223.0 4.2 reshape.270
  227.2 19.3 %all_to_all.116 = f32[128,1,1024]{2,1,0:T(1,128)} all-to-all(f32[128,1,1024]{2,1,0:T(1,128)} %reshape.270), channel_id=1, replica_groups=mesh['px'=8,'py'=16] {'px','py'}, dimensions={0} | all-to-all | bytes 1048576 | tf_op jit(solution)/shard_map/all_to_all | solution.py:58
  253.9 4.4 copy.119
  278.5 4.2 scatter_custom_fusion.4
  293.1 4.2 copy.202
  297.2 4.2 reshape.272
  301.4 19.2 %all_to_all.117 = f32[128,1,1024]{2,1,0:T(1,128)} all-to-all(f32[128,1,1024]{2,1,0:T(1,128)} %reshape.272), channel_id=1, replica_groups=mesh['px'=8,'py'=16] {'px','py'}, dimensions={0} | all-to-all | bytes 1048576 | tf_op jit(solution)/shard_map/all_to_all | solution.py:61
  327.9 4.4 copy.130
  346.1 62.9 %all-reduce = (f32[]{:T(128)}, f32[]{:T(128)}) all-reduce(f32[]{:T(128)} %get-tuple-element.3, f32[]{:T(128)} %get-tuple-element.2), channel_id=1, replica_groups=mesh['px'=8,'py'=16] {'px','py'}, use_global_device_ids=true, to_apply=%region_7.8 | all-reduce | flops 2 | bytes 16 | tf_op jit(solution)/shard_map/psum | solution.py:98
  412.2 62.7 %psum.30 = f32[]{:T(128)} all-reduce(f32[]{:T(128)} %multiply_reduce_fusion.1), channel_id=1, replica_groups=mesh['px'=8,'py'=16] {'px','py'}, use_global_device_ids=true, to_apply=%region_12.13 | all-reduce | flops 1 | bytes 8 | tf_op jit(solution)/shard_map/psum | solution.py:98
  482.1 4.2 copy.209
  489.8 19.3 %all_to_all.118 = f32[128,1,1024]{2,1,0:T(1,128)S(1)} all-to-all(f32[128,1,1024]{2,1,0:T(1,128)S(1)} %reshape.274), channel_id=1, replica_groups=mesh['px'=8,'py'=16] {'px','py'}, dimensions={0} | all-to-all | bytes 1048576 | tf_op jit(solution)/shard_map/all_to_all | solution.py:58
  513.7 4.4 copy.139
  537.1 4.0 scatter_custom_fusion.5
  553.7 17.9 %all_to_all.119 = f32[128,1,1024]{2,1,0:T(1,128)S(1)} all-to-all(f32[128,1,1024]{2,1,0:T(1,128)S(1)} %reshape.276), channel_id=1, replica_groups=mesh['px'=8,'py'=16] {'px','py'}, dimensions={0} | all-to-all | bytes 1048576 | tf_op jit(solution)/shard_map/all_to_all | solution.py:61
  576.1 4.4 copy.150
  591.0 62.7 %psum.31 = f32[]{:T(128)} all-reduce(f32[]{:T(128)} %get-tuple-element.6), channel_id=1, replica_groups=mesh['px'=8,'py'=16] {'px','py'}, use_global_device_ids=true, to_apply=%region_15.16 | all-reduce | flops 1 | bytes 8 | tf_op jit(solution)/shard_map/psum | solution.py:98
  (182 shorter events, 227.7 us)
Async XLA Ops:
  0.6 89.3 %copy-start = (f32[16,64]{1,0:T(8,128)S(1)}, f32[16,64]{1,0:T(8,128)}, u32[]{:S(2)}) copy-start(f32[16,64]{1,0:T(8,128)} %param.10) | copy-start | bytes 12292
  0.6 18.6 %copy-start.25 = (f32[16,64]{1,0:T(8,128)S(1)}, f32[16,64]{1,0:T(8,128)}, u32[]{:S(2)}) copy-start(f32[16,64]{1,0:T(8,128)} %param.9) | copy-start | bytes 12292
  5.0 21.3 %all-to-all-start = ((s32[128,2,1]{1,2,0:T(1,128)}), s32[128,2,1]{1,2,0:T(1,128)S(1)}, u32[]{:S(2)}, u32[]{:S(2)}) async-start(s32[128,2,1]{1,2,0:T(1,128)} %bitcast.6), calls=%async_computation | async-start | bytes 131072 | tf_op jit(solution)/shard_map/all_to_all | solution.py:87
  17.6 3.7 copy-start.24
  26.2 6.9 %copy-start.23 = (s32[128,2,1]{1,2,0:T(1,128)}, s32[128,2,1]{1,2,0:T(1,128)S(1)}, u32[]{:S(2)}) copy-start(s32[128,2,1]{1,2,0:T(1,128)S(1)} %all-to-all-done) | copy-start | bytes 3076
  26.2 18.4 %all-to-all-start.3 = ((bf16[128,2,431]{2,1,0:T(2,128)(2,1)}), bf16[128,2,431]{2,1,0:T(2,128)(2,1)S(1)}, u32[]{:S(2)}, u32[]{:S(2)}) async-start(bf16[128,2,431]{2,1,0:T(2,128)(2,1)} %all_to_all.90), calls=%async_computation.3 | async-start | bytes 524288 | tf_op jit(solution)/shard_map/all_to_all | solution.py:86
  44.6 34.3 %all-to-all-start.2 = ((f32[128,1,1024]{2,1,0:T(1,128)}), f32[128,1,1024]{2,1,0:T(1,128)S(1)}, u32[]{:S(2)}, u32[]{:S(2)}) async-start(f32[128,1,1024]{2,1,0:T(1,128)} %reshape.266), calls=%async_computation.2 | async-start | bytes 1048576 | tf_op jit(solution)/shard_map/all_to_all | solution.py:58
  78.9 0.8 copy-start.22
  79.7 60.9 %all-to-all-start.1 = ((bf16[256,16,431]{2,1,0:T(8,128)(2,1)}), bf16[256,16,431]{2,1,0:T(8,128)(2,1)}, u32[]{:S(2)}, u32[]{:S(2)}) async-start(bf16[256,16,431]{2,1,0:T(8,128)(2,1)} %scatter_fusion), calls=%async_computation.1 | async-start | bytes 8388608 | tf_op jit(solution)/shard_map/all_to_all | solution.py:85
  117.1 1.9 copy-start.2
  117.1 1.9 copy-start.12
  140.6 2.9 copy-start.21
  140.6 3.0 copy-start.26
  155.9 1.9 copy-start.10
  169.4 20.4 %all-to-all-start.4 = ((f32[128,1,1024]{2,1,0:T(1,128)}), f32[128,1,1024]{2,1,0:T(1,128)}, u32[]{:S(2)}, u32[]{:S(2)}) async-start(f32[128,1,1024]{2,1,0:T(1,128)} %reshape.268), calls=%async_computation.4 | async-start | bytes 1048576 | tf_op jit(solution)/shard_map/all_to_all | solution.py:61
  205.0 2.7 copy-start.5
  205.1 2.7 copy-start.16
  263.3 2.0 copy-start.3
  263.3 2.0 copy-start.15
  287.8 2.0 copy-start.11
  335.9 3.0 copy-start.6
  335.9 3.0 copy-start.17
  477.6 0.8 copy-start.18
  520.9 0.8 copy-start.13
  521.8 2.0 copy-start.4
  521.8 2.0 copy-start.14
  583.4 1.4 copy-start.7
  584.8 4.6 copy-start.19
  588.1 66.9 %copy-start.8 = (f32[16,8,1024]{2,1,0:T(8,128)S(1)}, f32[16,8,1024]{2,1,0:T(8,128)}, u32[]{:S(2)}) copy-start(f32[16,8,1024]{2,1,0:T(8,128)} %get-tuple-element.9) | copy-start | bytes 1572868
  588.1 66.9 %copy-start.9 = (f32[16,8,1024]{2,1,0:T(8,128)S(1)}, f32[16,8,1024]{2,1,0:T(8,128)}, u32[]{:S(2)}) copy-start(f32[16,8,1024]{2,1,0:T(8,128)} %reshape.141) | copy-start | bytes 1572868
  588.1 66.9 %copy-start.20 = (f32[16,8,1024]{2,1,0:T(8,128)S(1)}, f32[16,8,1024]{2,1,0:T(8,128)}, u32[]{:S(2)}) copy-start(f32[16,8,1024]{2,1,0:T(8,128)} %param.8) | copy-start | bytes 1572868
  589.4 67.9 %copy-start.1 = (f32[16,64]{1,0:T(8,128)S(1)}, f32[16,64]{1,0:T(8,128)}, u32[]{:S(2)}) copy-start(f32[16,64]{1,0:T(8,128)} %param.10) | copy-start | bytes 12292
where the time goes:
time: 669 us; the launch traced here: 658 us
  blocking collectives  264 us (39%)
  local copies, waits for them, and re-layouts  200 us (30%)
  matrix products  65.8 us (10%)
  other arithmetic  48.9 us (7%)
  starting transfers between devices  44.7 us (7%)
  waiting for transfers between devices  28.3 us (4%)
    psum x3, blocking collectives, inner(): return lax.psum(jnp.sum(first * second), ('px', 'py'))  188 us
    unnamed x71, local copies, waits for them, and re-layouts  54.2 us
    all_to_all x2, blocking collectives, to_columns(): lax.all_to_all(row_major, ('px', 'py'), split_axis=1, concat_axis=2, tile...  38.7 us
    all_to_all x2, blocking collectives, to_rows(): lax.all_to_all(column_major, ('px', 'py'), split_axis=1, concat_axis=2, t...  37 us
    reshape x6, local copies, waits for them, and re-layouts, convolve(): return result.reshape(levels, length, row_count)  22.9 us
    slice x24, local copies, waits for them, and re-layouts, convolve(): before = jnp.roll(blocks, 1, axis=2)[..., 128 - half_span:]  21.2 us
    reshape x6, local copies, waits for them, and re-layouts, convolve(): blocks = grid_field.reshape(levels, row_count, block_count, 128)  19.9 us
    dot_general x6, matrix products, convolve(): jnp.einsum('lrbj,lji->lbir', window, banded, precision=lax.Precision.HIGH...  19.4 us
  transfers between devices with their start and end apart: 5, of which 4 were waited for; matrix products, arithmetic and copies ran while one was open for 12% of the time, Pallas kernels for 0%

commit v1 on v0

v1 whole, which is shorter than its diff:
```python
import functools

import jax
import jax.numpy as jnp
from jax import lax
from jax.experimental import pallas as pl
from jax.experimental.pallas import tpu as pltpu
from jax.sharding import PartitionSpec as P

F32, BF16, I32 = jnp.float32, jnp.bfloat16, jnp.int32
MESH = pl.DeviceIdType.MESH
ND, NPX, NPY = 128, 8, 16
LEV, CH, TAPS = 16, 431, 64
NEAR = 17
MIDDLE = 8
FX, BX, FY, BY = range(4)
NT = (((1,), (1,)), ((), ()))
NN = (((1,), (0,)), ((), ()))
HIGHEST = lax.Precision.HIGHEST


def iota(shape, axis):
    return lax.broadcasted_iota(I32, shape, axis)


def split(values):
    high = values.astype(BF16)
    low = (values - high.astype(F32)).astype(BF16)
    return high, low


def stacked(values):
    return jnp.concatenate(split(values), axis=0)


def dot(left, right, dims=NN, precision=None):
    return lax.dot_general(left, right, dims, precision=precision, preferred_element_type=F32)


def swap_groups(tiles):
    group = iota((8, 128), 1) // 8
    tiles = list(tiles)
    for bit in range(4):
        step = 1 << bit
        upper = (group & step) != 0
        for a in range(16):
            if a & step == 0:
                first, second = tiles[a], tiles[a + step]
                tiles[a] = jnp.where(upper, pltpu.roll(second, 8 * step, 1), first)
                tiles[a + step] = jnp.where(upper, second, pltpu.roll(first, 128 - 8 * step, 1))
    return tiles


def spread_levels(values):
    count = values.shape[1]
    return jnp.broadcast_to(values[:, None, :], (LEV, 8, count)).reshape(LEV * 8, count)


def kernel(
    c0_ref, kx_ref, ky_ref, w_ref, jac_ref, innov_ref, dest_ref, cell_ref,
    control_ref, residual_ref,
    jac, innov, innov_wide, line, table, mixed, pad_a, pad_b, send_g, recv_g, pack, send_m, recv_m,
    model, extra, onehot, autocov, near_x, place, cells, queue_a, queue_b, recv_a, recv_b,
    field, high_field, part, sums_x, sums_y, send_f, recv_f,
    load_sem, dense_send, dense_recv, model_send, model_recv, cell_send, cell_recv,
    qa_send, qa_recv, qb_send, qb_recv, sx_send, sx_recv, sy_send, sy_recv, final_send, final_recv,
):
    my_x, my_y = lax.axis_index("px"), lax.axis_index("py")
    me = my_x * NPY + my_y

    def device(index):
        return (index // NPY, index % NPY)

    load_jac = pltpu.make_async_copy(jac_ref, jac, load_sem.at[0])
    load_innov = pltpu.make_async_copy(innov_ref, innov, load_sem.at[1])
    load_jac.start()
    load_innov.start()

    barrier = pltpu.get_barrier_semaphore()

    @pl.loop(1, ND)
    def _(step):
        pl.semaphore_signal(
            barrier, inc=1, device_id=device(lax.rem(me + step, ND)), device_id_type=MESH
        )

    tap = iota((TAPS, 128), 0)
    place_at = iota((TAPS, 128), 1)
    pick_forward = (tap == ((32 - place_at) & 127)).astype(F32)
    pick_backward = (tap == ((place_at + 32) & 127)).astype(F32)
    for which, (taps_ref, pick) in enumerate(
        ((kx_ref, pick_forward), (kx_ref, pick_backward), (ky_ref, pick_forward), (ky_ref, pick_backward))
    ):
        line[which] = dot(taps_ref[...], pick, precision=HIGHEST)

    inside = jnp.abs(iota((128, 128), 0) - iota((128, 128), 1)) < 64

    def circulant(row):
        return pltpu.roll(jnp.broadcast_to(row, (128, 128)), 0, 1, stride=1, stride_axis=0)

    def build_table(which):
        @pl.loop(0, LEV)
        def _(level):
            ring = circulant(line[which, pl.ds(level, 1), :])
            both = jnp.concatenate([jnp.where(inside, ring, 0.0), jnp.where(inside, 0.0, ring)], axis=0)
            high, low = split(both)
            table[which, level] = jnp.concatenate([high, low], axis=1)

    lower_half = iota((64, 128), 1) < 64

    def convolve(own, before, after, which, level):
        count = own.shape[0]
        beside = jnp.where(iota((count, 128), 1) < 64, after, before)
        product = dot(stacked(jnp.concatenate([own, beside], axis=1)), table[which, level])
        upper, lower = product[:count], product[count:]
        return (upper[:, :128] + upper[:, 128:]) + (lower[:, :128] + lower[:, 128:])

    build_table(FX)

    @pl.loop(0, LEV)
    def _(level):
        blocks = [c0_ref[level, :, 128 * b : 128 * b + 128] for b in range(8)]
        own = jnp.concatenate(blocks, axis=0)
        before = jnp.concatenate(blocks[7:] + blocks[:7], axis=0)
        after = jnp.concatenate(blocks[1:] + blocks[:1], axis=0)
        out = convolve(own, before, after, FX, level)
        for b in range(8):
            mixed[b, level] = out[8 * b : 8 * b + 8]

    @pl.loop(0, 8)
    def _(block):
        tiles = swap_groups([mixed[block, level] for level in range(LEV)])
        for j in range(16):
            send_g[pl.ds(pl.multiple_of(128 * block + 8 * j, 8), 8), :] = tiles[j]

    pl.semaphore_wait(barrier, ND - 1)

    def exchange(source, target, rows, send_sem, recv_sem):
        mine = pl.ds(pl.multiple_of(me * rows, rows), rows)

        @pl.loop(1, ND)
        def _(step):
            other = lax.rem(me + step, ND)
            pltpu.make_async_remote_copy(
                src_ref=source.at[pl.ds(pl.multiple_of(other * rows, rows), rows)],
                dst_ref=target.at[mine],
                send_sem=send_sem,
                recv_sem=recv_sem,
                device_id=device(other),
                device_id_type=MESH,
            ).start()

        target[mine, :] = source[mine, :]
        whole = pl.ds(0, (ND - 1) * rows)
        return pltpu.make_async_remote_copy(
            src_ref=source.at[whole],
            dst_ref=target.at[whole],
            send_sem=send_sem,
            recv_sem=recv_sem,
            device_id=device(lax.rem(me + 1, ND)),
            device_id_type=MESH,
        )

    dense = exchange(send_g, recv_g, 8, dense_send, dense_recv)

    load_jac.wait()
    load_innov.wait()
    innov_wide[...] = innov[...].astype(F32)

    def one_channel(channel, carry):
        values = jac[channel].astype(F32)
        scaled = values * w_ref[channel]
        matrix, rhs = carry
        matrix = tuple(
            m + scaled * jnp.broadcast_to(values[k : k + 1], (LEV, 128)) for k, m in enumerate(matrix)
        )
        return matrix, rhs + scaled * jnp.broadcast_to(innov_wide[pl.ds(channel, 1), :], (LEV, 128))

    zero = jnp.zeros((LEV, 128), F32)
    matrix, rhs = lax.fori_loop(0, CH, one_channel, ((zero,) * LEV, zero))
    for k in range(LEV):
        pack[16 * k : 16 * k + 16, :] = matrix[k]
    pack[256:272, :] = rhs
    pack[272:384, :] = jnp.zeros((112, 128), F32)
    pack[272:273, :] = cell_ref[...].astype(F32) + 1.0

    dest = jnp.broadcast_to(dest_ref[...], (128, 128))
    dest_t = jnp.transpose(dest.astype(F32))
    earlier = (dest.astype(F32) == dest_t) & (iota((128, 128), 0) < iota((128, 128), 1))
    rank = jnp.sum(earlier.astype(F32), axis=0, keepdims=True)
    named = iota((128, 128), 0) == dest
    chosen = jnp.concatenate(
        [(named & (rank == float(k))).astype(BF16) for k in range(2)], axis=0
    )
    pack_high, pack_low = split(pack[...])
    packed = dot(chosen, pack_high, NT) + dot(chosen, pack_low, NT)
    send_m[...] = jnp.zeros_like(send_m)
    for k in range(2):
        for i in range(3):
            send_m[pl.ds(4 * k + i, 128, stride=8), :] = packed[128 * k : 128 * k + 128, 128 * i : 128 * i + 128]

    models = exchange(send_m, recv_m, 8, model_send, model_recv)

    build_table(FY)
    build_table(BY)
    build_table(BX)

    column = iota((8, 128), 1)
    offset = iota((8, 128), 0)

    @pl.loop(0, LEV)
    def _(level):
        taps = line[BX, pl.ds(level, 1), :]
        rows = jnp.broadcast_to(taps, (8, 128))
        cov = dot(rows, circulant(line[BX, pl.ds(level, 1), :]), NT, precision=HIGHEST)
        ring = pltpu.roll(cov, 64, 1, stride=1, stride_axis=0)
        at = pl.ds(pl.multiple_of(8 * level, 8), 8)
        autocov[0, at, :] = jnp.where(column > offset, ring, 0.0)
        autocov[1, at, :] = jnp.where(column < offset, ring, 0.0)

    for block in (0, 9):
        pad_a[:, 8 * block : 8 * block + 8, :] = jnp.zeros((LEV, 8, 128), F32)
        pad_b[:, 8 * block : 8 * block + 8, :] = jnp.zeros((LEV, 8, 128), F32)

    def along_rows(source, which, level):
        return convolve(
            source[level, 8:72, :], source[level, 0:64, :], source[level, 16:80, :], which, level
        )

    dense.wait_recv()

    @pl.loop(0, 8)
    def _(block):
        turned = jnp.transpose(recv_g[pl.ds(pl.multiple_of(128 * block, 128), 128), :])
        pad_a[:, pl.ds(pl.multiple_of(8 + 8 * block, 8), 8), :] = turned.reshape(LEV, 8, 128)

    def filter_to_field(source):
        @pl.loop(0, LEV)
        def _(level):
            out = along_rows(source, FY, level)
            at = pl.ds(pl.multiple_of(8 * level, 8), 8)
            for b in range(8):
                high_field[at, 128 * b : 128 * b + 128] = out[8 * b : 8 * b + 8]

    filter_to_field(pad_a)

    models.wait_recv()
    for k in range(2):
        lanes = slice(128 * k, 128 * k + 128)
        for i in range(2):
            turned = jnp.transpose(recv_m[pl.ds(4 * k + i, 128, stride=8), :])
            model[8 * i : 8 * i + 8, :, lanes] = turned.reshape(8, LEV, 128)
        turned = jnp.transpose(recv_m[pl.ds(4 * k + 2, 128, stride=8), :])
        extra[0:24, lanes] = turned[0:24]
    code = extra[16:17, :] - 1.0
    cell_x = jnp.floor(code * (1.0 / 1024.0))
    cell_y = jnp.where(code < 0.0, -1.0, code - 1024.0 * cell_x)
    cells[...] = jnp.concatenate([cell_x, cell_y, jnp.zeros((6, 256), F32)], axis=0)
    place[MIDDLE] = cells[...]

    def neighbour_copy(source, target, send_sem, recv_sem, slot):
        other = lax.rem(me - (slot - MIDDLE) + ND, ND)
        return pltpu.make_async_remote_copy(
            src_ref=source,
            dst_ref=target.at[slot],
            send_sem=send_sem.at[slot],
            recv_sem=recv_sem.at[slot],
            device_id=device(other),
            device_id_type=MESH,
        )

    def for_neighbours(action):
        @pl.loop(0, NEAR - 1)
        def _(index):
            action(index + (index >= MIDDLE).astype(I32))

    for_neighbours(lambda slot: neighbour_copy(cells, place, cell_send, cell_recv, slot).start())

    row_number = iota((128, 256), 0).astype(F32)

    def build_onehot(slot):
        row_of = place[slot, 1:2, :]

        @pl.loop(0, 8)
        def _(block):
            base = (128 * block).astype(F32)
            hit = (row_number + base) == row_of
            onehot[slot, pl.ds(pl.multiple_of(128 * block, 128), 128), :] = hit.astype(BF16)

        column_of = place[slot, 0:1, :]
        wraps = slot == NEAR - 1
        first = jnp.where(wraps, 0, 8 * slot).astype(F32)
        hit = (row_number == column_of + first).astype(BF16)
        product = dot(stacked(autocov[jnp.where(wraps, 1, 0)]), hit)
        near_x[slot] = product[:128] + product[128:]

    build_onehot(MIDDLE)
    own_column = jnp.broadcast_to(place[MIDDLE, 0:1, :], (8, 256)) == iota((8, 256), 0).astype(F32)

    def sample():
        high, low = split(high_field[...])
        product = dot(high, onehot[MIDDLE]) + dot(low, onehot[MIDDLE])
        return jnp.sum(jnp.where(own_column[None], product.reshape(LEV, 8, 256), 0.0), axis=1)

    def apply_model(values):
        total = jnp.zeros((LEV, 256), F32)
        for k in range(LEV):
            total = total + model[k] * jnp.broadcast_to(values[k : k + 1], (LEV, 256))
        return total

    z0 = sample()
    q1 = apply_model(z0) - extra[0:16, :]
    queue_a[...] = q1
    recv_a[MIDDLE] = q1
    for_neighbours(lambda slot: neighbour_copy(queue_a, recv_a, qa_send, qa_recv, slot).start())

    def arrive_cells(slot):
        neighbour_copy(cells, place, cell_send, cell_recv, slot).wait_recv()
        build_onehot(slot)

    for_neighbours(arrive_cells)

    def covary(source, target, send_sem, recv_sem):
        field[...] = jnp.zeros_like(field)

        def add(slot):
            spread = near_x[slot] * spread_levels(target[slot])
            pair = stacked(spread)

            @pl.loop(0, 4)
            def _(quarter):
                at = pl.ds(pl.multiple_of(256 * quarter, 256), 256)
                field[quarter] += dot(pair, onehot[slot, at, :], NT)

        add(MIDDLE)

        def arrived(slot):
            neighbour_copy(source, target, send_sem, recv_sem, slot).wait_recv()
            add(slot)

        for_neighbours(arrived)
        fill_pad(field)

        @pl.loop(0, LEV)
        def _(level):
            pad_b[level, 8:72, :] = along_rows(pad_a, BY, level)

        filter_to_field(pad_b)
        return sample()

    def fill_pad(source):
        @pl.loop(0, 4)
        def _(quarter):
            total = source[quarter, 0:128, :] + source[quarter, 128:256, :]
            for half in range(2):
                rows = pl.ds(pl.multiple_of(8 + 16 * quarter + 8 * half, 8), 8)
                pad_a[:, rows, :] = total[:, 128 * half : 128 * half + 128].reshape(LEV, 8, 128)

    t1 = covary(queue_a, recv_a, qa_send, qa_recv)
    s0 = -(z0 + t1)
    q2 = apply_model(s0)
    queue_b[...] = q2
    recv_b[MIDDLE] = q2
    for_neighbours(lambda slot: neighbour_copy(queue_b, recv_b, qb_send, qb_recv, slot).start())
    t2 = covary(queue_b, recv_b, qb_send, qb_recv)
    u = apply_model(t2)

    def partial(first, second):
        product = jnp.sum(first * second, axis=0, keepdims=True)
        return product[:, :128] + product[:, 128:]

    start = jnp.sum(jnp.sum((c0_ref[...] * c0_ref[...]).reshape(LEV * 8, 1024), axis=0, keepdims=True).reshape(8, 128), axis=0, keepdims=True)
    part[...] = jnp.concatenate(
        [start, partial(z0, q1), partial(q1, t1), partial(s0, q2), partial(t2, q2), partial(t2, u),
         jnp.zeros((2, 128), F32)], axis=0)

    def sum_over(source, target, count, mine, other_of, send_sem, recv_sem):
        @pl.loop(1, count)
        def _(step):
            pltpu.make_async_remote_copy(
                src_ref=source,
                dst_ref=target.at[mine],
                send_sem=send_sem,
                recv_sem=recv_sem,
                device_id=other_of(lax.rem(mine + step, count)),
                device_id_type=MESH,
            ).start()

        target[mine] = source[...]
        whole = pltpu.make_async_remote_copy(
            src_ref=target.at[pl.ds(0, count - 1)],
            dst_ref=target.at[pl.ds(0, count - 1)],
            send_sem=send_sem,
            recv_sem=recv_sem,
            device_id=other_of(lax.rem(mine + 1, count)),
            device_id_type=MESH,
        )
        whole.wait_recv()
        whole.wait_send()
        return jnp.sum(target[...], axis=0)

    part_x = sum_over(part, sums_x, NPX, my_x, lambda o: (o, my_y), sx_send, sx_recv)
    part[...] = part_x
    total = sum_over(part, sums_y, NPY, my_y, lambda o: (my_x, o), sy_send, sy_recv)
    scalar = jnp.sum(total, axis=1, keepdims=True)
    c0c0, z0q1, q1t1, s0q2, q2t2, t2u = [scalar[k : k + 1] for k in range(6)]
    norm0 = c0c0 + 2.0 * z0q1 + q1t1
    alpha0 = norm0 / (norm0 + s0q2)
    keep = 1.0 - alpha0
    norm1 = keep * keep * norm0 - 2.0 * alpha0 * keep * s0q2 + alpha0 * alpha0 * q2t2
    beta0 = norm1 / norm0
    gain = keep + beta0
    curvature = gain * gain * s0q2 - 2.0 * gain * alpha0 * q2t2 + alpha0 * alpha0 * t2u
    alpha1 = norm1 / (norm1 + beta0 * beta0 * norm0 + curvature)
    coef_c = alpha0 + alpha1 * gain
    coef_r = (1.0 - alpha1) * keep - alpha1 * beta0
    y_control = coef_c * q1 + (alpha0 * alpha1) * q2
    y_residual = coef_r * q1 + ((1.0 - alpha1) * alpha0) * q2 + alpha1 * (gain * q2 - alpha0 * u)

    own_mask = jnp.broadcast_to(own_column[None], (LEV, 8, 256)).reshape(LEV * 8, 256)

    for index, values in enumerate((y_control, y_residual)):
        pair = stacked(jnp.where(own_mask, spread_levels(values), 0.0))

        @pl.loop(0, 4)
        def _(quarter):
            at = pl.ds(pl.multiple_of(256 * quarter, 256), 256)
            field[quarter] = dot(pair, onehot[MIDDLE, at, :], NT)

        fill_pad(field)

        @pl.loop(0, LEV)
        def _(level):
            out = along_rows(pad_a, BY, level)
            for b in range(8):
                mixed[8 * index + b, level] = out[8 * b : 8 * b + 8]

    @pl.loop(0, 8)
    def _(block):
        first = swap_groups([mixed[block, level] for level in range(LEV)])
        second = swap_groups([mixed[8 + block, level] for level in range(LEV)])
        for j in range(16):
            at = pl.ds(pl.multiple_of(256 * block + 16 * j, 16), 16)
            send_f[at, :] = jnp.concatenate([first[j], second[j]], axis=0).astype(BF16)

    final = exchange(send_f, recv_f, 16, final_send, final_recv)
    final.wait_recv()

    @pl.loop(0, 8)
    def _(block):
        arrived = recv_f[pl.ds(pl.multiple_of(256 * block, 256), 256), :].astype(F32)
        arrived = arrived.reshape(16, 2, 8, 128)
        for index in range(2):
            turned = jnp.transpose(arrived[:, index].reshape(128, 128))
            mixed[8 * index + block] = turned.reshape(LEV, 8, 128)

    for index, (out_ref, coef) in enumerate(((control_ref, 1.0 - coef_c), (residual_ref, -coef_r))):
        @pl.loop(0, LEV)
        def _(level):
            blocks = [mixed[8 * index + b, level] for b in range(8)]
            own = jnp.concatenate(blocks, axis=0)
            before = jnp.concatenate(blocks[7:] + blocks[:7], axis=0)
            after = jnp.concatenate(blocks[1:] + blocks[:1], axis=0)
            out = convolve(own, before, after, BX, level)
            for b in range(8):
                lanes = slice(128 * b, 128 * b + 128)
                out_ref[level, :, lanes] = coef * c0_ref[level, :, lanes] - out[8 * b : 8 * b + 8]

    dense.wait_send()
    models.wait_send()
    final.wait_send()

    def sent(slot):
        neighbour_copy(cells, place, cell_send, cell_recv, slot).wait_send()
        neighbour_copy(queue_a, recv_a, qa_send, qa_recv, slot).wait_send()
        neighbour_copy(queue_b, recv_b, qb_send, qb_recv, slot).wait_send()

    for_neighbours(sent)


def per_device(
    control_init, kernel_x, kernel_y, obs_weight, jacobian, innovation, obs_dest, obs_cell
):
    vmem = pl.BlockSpec(memory_space=pltpu.VMEM)
    anywhere = pl.BlockSpec(memory_space=pl.ANY)
    shape = jax.ShapeDtypeStruct(control_init.shape, F32)
    dma = pltpu.SemaphoreType.DMA
    return pl.pallas_call(
        kernel,
        out_shape=(shape, shape),
        in_specs=[vmem, vmem, vmem, pl.BlockSpec(memory_space=pltpu.SMEM), anywhere, anywhere, vmem, vmem],
        out_specs=(vmem, vmem),
        scratch_shapes=[
            pltpu.VMEM((CH, LEV, 128), BF16),
            pltpu.VMEM((CH, 128), BF16),
            pltpu.VMEM((CH, 128), F32),
            pltpu.VMEM((4, LEV, 128), F32),
            pltpu.VMEM((4, LEV, 256, 256), BF16),
            pltpu.VMEM((16, LEV, 8, 128), F32),
            pltpu.VMEM((LEV, 80, 128), F32),
            pltpu.VMEM((LEV, 80, 128), F32),
            pltpu.VMEM((1024, 128), F32),
            pltpu.VMEM((1024, 128), F32),
            pltpu.VMEM((384, 128), F32),
            pltpu.VMEM((1024, 128), F32),
            pltpu.VMEM((1024, 128), F32),
            pltpu.VMEM((LEV, LEV, 256), F32),
            pltpu.VMEM((24, 256), F32),
            pltpu.VMEM((NEAR, 1024, 256), BF16),
            pltpu.VMEM((2, 128, 128), F32),
            pltpu.VMEM((NEAR, 128, 256), F32),
            pltpu.VMEM((NEAR, 8, 256), F32),
            pltpu.VMEM((8, 256), F32),
            pltpu.VMEM((LEV, 256), F32),
            pltpu.VMEM((LEV, 256), F32),
            pltpu.VMEM((NEAR, LEV, 256), F32),
            pltpu.VMEM((NEAR, LEV, 256), F32),
            pltpu.VMEM((4, 256, 256), F32),
            pltpu.VMEM((128, 1024), F32),
            pltpu.VMEM((8, 128), F32),
            pltpu.VMEM((NPX, 8, 128), F32),
            pltpu.VMEM((NPY, 8, 128), F32),
            pltpu.VMEM((2048, 128), BF16),
            pltpu.VMEM((2048, 128), BF16),
            dma((2,)),
            dma, dma, dma, dma,
            dma((NEAR,)), dma((NEAR,)),
            dma((NEAR,)), dma((NEAR,)), dma((NEAR,)), dma((NEAR,)),
            dma, dma, dma, dma, dma, dma,
        ],
        compiler_params=pltpu.CompilerParams(
            collective_id=0, has_side_effects=True, vmem_limit_bytes=52 * 1024 * 1024
        ),
    )(
        control_init,
        kernel_x,
        kernel_y,
        obs_weight,
        jnp.transpose(jacobian, (2, 1, 0)),
        jnp.transpose(innovation),
        jnp.transpose(obs_dest),
        obs_cell.reshape(1, -1),
    )


def solution(mesh):
    in_specs = (
        P(None, ("px", "py"), None),
        P(),
        P(),
        P(),
        P(("px", "py"), None, None),
        P(("px", "py"), None),
        P(("px", "py"), None),
        P(("px", "py")),
    )
    out_specs = (P(None, ("px", "py"), None), P(None, ("px", "py"), None))
    return jax.shard_map(
        per_device, mesh=mesh, in_specs=in_specs, out_specs=out_specs, check_vma=False
    )
```

time: 669 us -> 145 us (0.22); the launches traced: 658 us -> 144 us
  blocking collectives: 264 us -> 0 us
  local copies, waits for them, and re-layouts: 200 us -> 6.9 us
  Pallas kernels: 0 us -> 137 us
  matrix products: 65.8 us -> 0 us
  other arithmetic: 48.9 us -> 0 us
  starting transfers between devices: 44.7 us -> 0 us
  waiting for transfers between devices: 28.3 us -> 0 us
    psum x3 -> x0, blocking collectives: 188 us -> none  [inner(): return lax.psum(jnp.sum(first * second), ('px', 'py'))]
    pallas_call x0 -> x1, Pallas kernels: none -> 137 us  [per_device(): pl.pallas_call(kernel, out_shape=(shape, shape), in_specs=[vmem, vmem, vm...]
    all_to_all x4 -> x0, blocking collectives: 75.7 us -> none  [the longest x2 38.7 us: to_columns(): lax.all_to_all(row_major, ('px', 'py'), split_axis=1, concat_axis=2, tile...]
    dot_general x22 -> x0, matrix products: 65.8 us -> none  [the longest x6 19.4 us: convolve(): jnp.einsum('lrbj,lji->lbir', window, banded, precision=lax.Precision.HIGH...]
    reshape x15 -> x0, local copies, waits for them, and re-layouts: 47.8 us -> none  [the longest x6 22.9 us: convolve(): return result.reshape(levels, length, row_count)]
    unnamed x71 -> x16, local copies, waits for them, and re-layouts: 54.2 us -> 6.9 us
    all_to_all x5 -> x0, starting transfers between devices: 44.7 us -> none  [the longest x1 11.5 us: per_device(): lax.all_to_all(cell_slots, ('px', 'py'), split_axis=0, concat_axis=0, til...]
    all_to_all x11 -> x0, local copies, waits for them, and re-layouts: 30 us -> none  [the longest x4 13.7 us: to_columns(): lax.all_to_all(row_major, ('px', 'py'), split_axis=1, concat_axis=2, tile...]
  transfers between devices with their start and end apart: 5 -> 0, of which waited for: 4 -> 0; matrix products, arithmetic and copies ran while one was open for 12% -> 0% of each run, Pallas kernels for 0% -> 0%
where the time goes in v1:
time: 145 us; the launch traced here: 144 us
  Pallas kernels  137 us (94%)
  local copies, waits for them, and re-layouts  6.9 us (5%)
    pallas_call x1, Pallas kernels, per_device(): pl.pallas_call(kernel, out_shape=(shape, shape), in_specs=[vmem, vmem, vm...  137 us
    unnamed x16, local copies, waits for them, and re-layouts  6.9 us

profile of v1, /device:TPU:1, one launch (start us, length us, event | category | flops | bytes accessed | tf_op | source)
XLA Modules:
  0.0 144.3 jit_solution(6643159306575486325)
XLA Ops:
  0.6 0.0 copy-start
  0.6 1.0 copy-done
  1.7 0.0 copy-start.1
  1.7 0.9 copy-done.1
  2.6 0.0 copy-start.2
  2.6 0.7 copy-done.2
  3.3 0.0 copy-start.3
  3.3 0.7 copy-done.3
  4.0 0.0 copy-start.4
  4.0 0.7 copy-done.4
  4.6 0.0 copy-start.5
  4.7 0.7 copy-done.5
  5.3 0.0 copy-start.6
  5.3 0.7 copy-done.6
  6.0 136.7 %shard_map.95 = (f32[16,8,1024]{2,1,0:T(8,128)S(1)}, f32[16,8,1024]{2,1,0:T(8,128)S(1)}) custom-call(f32[16,8,1024]{2,1,0:T(8,128)S(1)} %copy-done, f32[16,64]{1,0:T(8,128)S(1)} %copy-done.2, f32[16,64]{1,0:T(8,128)S(1)} %copy-done.3, f32[431]{0:T(512)S(1)} %copy-done.4, bf16[431,16,128]{2,1,0:T(8,128)(2,1)} %bitcast.7, bf16[431,128]{1,0:T(8,128)(2,1)S(1)} %bitcast.4, ...), custom_call_target="tpu_custom_call" | custom-call | tf_op jit(solution)/shard_map/pallas_call | solution.py:488
  142.7 0.8 copy.12
  143.5 0.8 copy.13
Async XLA Ops:
  0.6 1.0 copy-start
  1.7 0.9 copy-start.1
  2.6 0.7 copy-start.2
  3.3 0.7 copy-start.3
  4.0 0.7 copy-start.4
  4.6 0.7 copy-start.5
  5.3 0.7 copy-start.6

commit v2 on v1

v2 whole, which is shorter than its diff:
```python
import functools

import jax
import jax.numpy as jnp
from jax import lax
from jax.experimental import pallas as pl
from jax.experimental.pallas import tpu as pltpu
from jax.sharding import PartitionSpec as P

F32, BF16, I32 = jnp.float32, jnp.bfloat16, jnp.int32
MESH = pl.DeviceIdType.MESH
ND, NPX, NPY = 128, 8, 16
LEV, CH, TAPS = 16, 431, 64
NEAR = 17
MIDDLE = 8
REACH = NEAR * 256
FX, BX, FY, BY = range(4)
NT = (((1,), (1,)), ((), ()))
NN = (((1,), (0,)), ((), ()))
HIGHEST = lax.Precision.HIGHEST


def iota(shape, axis):
    return lax.broadcasted_iota(I32, shape, axis)


def split(values):
    high = values.astype(BF16)
    low = (values - high.astype(F32)).astype(BF16)
    return high, low


def stacked(values):
    return jnp.concatenate(split(values), axis=0)


def dot(left, right, dims=NN, precision=None):
    return lax.dot_general(left, right, dims, precision=precision, preferred_element_type=F32)


def swap_groups(tiles):
    group = iota((8, 128), 1) // 8
    tiles = list(tiles)
    for bit in range(4):
        step = 1 << bit
        upper = (group & step) != 0
        for a in range(16):
            if a & step == 0:
                first, second = tiles[a], tiles[a + step]
                tiles[a] = jnp.where(upper, pltpu.roll(second, 8 * step, 1), first)
                tiles[a + step] = jnp.where(upper, second, pltpu.roll(first, 128 - 8 * step, 1))
    return tiles


def spread_levels(values):
    count = values.shape[1]
    return jnp.broadcast_to(values[:, None, :], (LEV, 8, count)).reshape(LEV * 8, count)


def kernel(
    c0_hbm, kx_hbm, ky_hbm, w_hbm, jac_hbm, innov_hbm, dest_hbm, cell_hbm,
    control_ref, residual_ref,
    c0_ref, kx_ref, ky_ref, w_ref, jac, innov, dest_ref, cell_ref,
    innov_wide, line, table, mixed, tile_m, send_g, recv_g, wide,
    model, extra, onehot, onehot_rows, autocov, near_x, place, cells, queue_a, queue_b,
    recv_a, recv_b, spread_q, grid, high_field, adjoint, part, sums, send_f, recv_f,
    load_sem, dense_send, dense_recv, cell_send, cell_recv,
    qa_send, qa_recv, qb_send, qb_recv, sum_send, sum_recv, final_send, final_recv,
):
    my_x, my_y = lax.axis_index("px"), lax.axis_index("py")
    me = my_x * NPY + my_y

    def device(index):
        return (index >> 4, index & 15)

    loads = [
        pltpu.make_async_copy(source, target, load_sem.at[i])
        for i, (source, target) in enumerate(
            (
                (c0_hbm, c0_ref), (kx_hbm, kx_ref), (ky_hbm, ky_ref), (w_hbm, w_ref),
                (jac_hbm, jac), (innov_hbm, innov), (dest_hbm, dest_ref), (cell_hbm, cell_ref),
            )
        )
    ]
    for load in loads:
        load.start()

    barrier = pltpu.get_barrier_semaphore()

    @pl.loop(1, ND)
    def _(step):
        pl.semaphore_signal(
            barrier, inc=1, device_id=device((me + step) & (ND - 1)), device_id_type=MESH
        )

    loads[1].wait()
    loads[2].wait()
    tap = iota((TAPS, 128), 0)
    place_at = iota((TAPS, 128), 1)
    pick_forward = (tap == ((32 - place_at) & 127)).astype(F32)
    pick_backward = (tap == ((place_at + 32) & 127)).astype(F32)
    for which, (taps_ref, pick) in enumerate(
        ((kx_ref, pick_forward), (kx_ref, pick_backward), (ky_ref, pick_forward), (ky_ref, pick_backward))
    ):
        line[which] = dot(taps_ref[...], pick, precision=HIGHEST)

    inside = jnp.abs(iota((128, 128), 0) - iota((128, 128), 1)) < 64

    def circulant(row):
        return pltpu.roll(jnp.broadcast_to(row, (128, 128)), 0, 1, stride=1, stride_axis=0)

    def build_table(which):
        @pl.loop(0, LEV, unroll=4)
        def _(level):
            ring = circulant(line[which, pl.ds(level, 1), :])
            high, low = split(ring)
            pair = jnp.concatenate([high, low], axis=1)
            nil = jnp.zeros((), BF16)
            keep = jnp.concatenate([inside, inside], axis=1)
            table[which, level, 0:128, :] = jnp.where(keep, pair, nil)
            table[which, level, 128:256, :] = jnp.where(keep, nil, pair)

    def convolve(own, before, after, which, level):
        count = own.shape[0]
        beside = jnp.where(iota((count, 128), 1) < 64, after, before)
        product = dot(stacked(jnp.concatenate([own, beside], axis=1)), table[which, level])
        upper, lower = product[:count], product[count:]
        return (upper[:, :128] + upper[:, 128:]) + (lower[:, :128] + lower[:, 128:])

    def along_x(own, which, level):
        before = jnp.concatenate([own[56:], own[:56]], axis=0)
        after = jnp.concatenate([own[8:], own[:8]], axis=0)
        return convolve(own, before, after, which, level)

    edge = jnp.zeros((8, 128), F32)

    def along_y(own, which, level):
        before = jnp.concatenate([edge, own[:56]], axis=0)
        after = jnp.concatenate([own[8:], edge], axis=0)
        return convolve(own, before, after, which, level)

    build_table(FX)
    loads[0].wait()

    for level in range(LEV):
        own = jnp.concatenate([c0_ref[level, :, 128 * b : 128 * b + 128] for b in range(8)], axis=0)
        out = along_x(own, FX, level)
        for b in range(8):
            mixed[b, level] = out[8 * b : 8 * b + 8]

    for load in loads[3:]:
        load.wait()
    innov_wide[...] = innov[...].astype(F32)

    def one_channel(channel, carry):
        values = jac[channel].astype(F32)
        scaled = values * w_ref[channel]
        matrix, rhs = carry
        matrix = tuple(
            m + scaled * jnp.broadcast_to(values[k : k + 1], (LEV, 128)) for k, m in enumerate(matrix)
        )
        return matrix, rhs + scaled * jnp.broadcast_to(innov_wide[pl.ds(channel, 1), :], (LEV, 128))

    def some_channels(index, carry):
        for k in range(8):
            carry = one_channel(8 * index + k, carry)
        return carry

    zero = jnp.zeros((LEV, 128), F32)
    carry = lax.fori_loop(0, CH // 8, some_channels, ((zero,) * LEV, zero))
    for channel in range(CH // 8 * 8, CH):
        carry = one_channel(channel, carry)
    matrix, rhs = carry

    cell = cell_ref[...]
    rhs_high, rhs_low = split(rhs)
    codes = jnp.concatenate([(cell >> 10) + 1, (cell & 1023) >> 3, cell & 7, jnp.zeros((93, 128), I32)], axis=0)
    pack = jnp.concatenate(
        [m.astype(BF16) for m in matrix] + [rhs_high, rhs_low, codes.astype(F32).astype(BF16)], axis=0
    )
    dest = jnp.broadcast_to(dest_ref[...], (128, 128))
    dest_t = jnp.transpose(dest.astype(F32))
    earlier = (dest.astype(F32) == dest_t) & (iota((128, 128), 0) < iota((128, 128), 1))
    rank = jnp.sum(earlier.astype(F32), axis=0, keepdims=True)
    named = iota((128, 128), 0) == dest
    chosen = jnp.concatenate([(named & (rank == float(k))).astype(BF16) for k in range(2)], axis=0)
    packed = dot(chosen, pack, NT)
    for k in range(2):
        for i in range(3):
            tile_m[pl.ds(3 * k + i, 128, stride=8), :] = packed[128 * k : 128 * k + 128, 128 * i : 128 * i + 128]
    for i in range(6, 8):
        tile_m[pl.ds(i, 128, stride=8), :] = jnp.zeros((128, 128), F32)

    @pl.loop(0, 8)
    def _(block):
        tiles = swap_groups([mixed[block, level] for level in range(LEV)])
        for j in range(16):
            lower = tile_m[pl.ds(pl.multiple_of(128 * block + 8 * j, 8), 8), :]
            at = pl.ds(pl.multiple_of(256 * block + 16 * j, 16), 16)
            send_g[at, :] = jnp.concatenate([tiles[j], lower], axis=0).astype(BF16)

    pl.semaphore_wait(barrier, ND - 1)

    def exchange(source, target, rows, source_of, send_sem, recv_sem):
        mine = pl.ds(pl.multiple_of(me * rows, rows), rows)

        @pl.loop(1, ND)
        def _(step):
            other = (me + step) & (ND - 1)
            pltpu.make_async_remote_copy(
                src_ref=source.at[source_of(other)],
                dst_ref=target.at[mine],
                send_sem=send_sem,
                recv_sem=recv_sem,
                device_id=device(other),
                device_id_type=MESH,
            ).start()

        target[mine, :] = source[source_of(me), :]
        whole = pl.ds(0, (ND - 1) * rows)
        return pltpu.make_async_remote_copy(
            src_ref=target.at[whole],
            dst_ref=target.at[whole],
            send_sem=send_sem,
            recv_sem=recv_sem,
            device_id=device((me + 1) & (ND - 1)),
            device_id_type=MESH,
        )

    def tile_of(index):
        return pl.ds(pl.multiple_of(index * 16, 16), 16)

    dense = exchange(send_g, recv_g, 16, tile_of, dense_send, dense_recv)

    build_table(FY)
    build_table(BY)
    build_table(BX)

    column = iota((8, 128), 1)
    offset = iota((8, 128), 0)

    @pl.loop(0, LEV, unroll=4)
    def _(level):
        taps = line[BX, pl.ds(level, 1), :]
        cov = dot(jnp.broadcast_to(taps, (8, 128)), circulant(taps), NT, precision=HIGHEST)
        ring = pltpu.roll(cov, 64, 1, stride=1, stride_axis=0)
        at = pl.ds(pl.multiple_of(8 * level, 8), 8)
        autocov[0, at, :] = jnp.where(column > offset, ring, 0.0)
        autocov[1, at, :] = jnp.where(column < offset, ring, 0.0)

    dense.wait_recv()

    for block in range(8):
        values = recv_g[256 * block : 256 * block + 256, :].astype(F32)
        wide[256 * block : 256 * block + 256, :] = values
        turned = jnp.transpose(values.reshape(16, 16, 128)[:, 0:8].reshape(128, 128))
        grid[:, 8 * block : 8 * block + 8, :] = turned.reshape(LEV, 8, 128)

    for k in range(2):
        lanes = slice(128 * k, 128 * k + 128)
        for i in range(2):
            turned = jnp.transpose(wide[pl.ds(8 + 3 * k + i, 128, stride=16), :])
            model[8 * i : 8 * i + 8, :, lanes] = turned.reshape(8, LEV, 128)
        turned = jnp.transpose(wide[pl.ds(8 + 3 * k + 2, 128, stride=16), :])
        extra[:, lanes] = turned[0:40]
        cell_x = turned[32:33] - 1.0
        cell_y = jnp.where(cell_x < 0.0, -1.0, 8.0 * turned[33:34] + turned[34:35])
        cells[k : k + 1, :] = cell_x
        cells[2 + k : 3 + k, :] = cell_y
    cells[4:8, :] = jnp.zeros((4, 128), F32)
    place[MIDDLE] = cells[...]

    def neighbour_copy(source, target, send_sem, recv_sem, slot):
        other = (me - (slot - MIDDLE)) & (ND - 1)
        return pltpu.make_async_remote_copy(
            src_ref=source,
            dst_ref=target.at[slot],
            send_sem=send_sem.at[slot],
            recv_sem=recv_sem.at[slot],
            device_id=device(other),
            device_id_type=MESH,
        )

    def for_neighbours(action, unroll=1):
        @pl.loop(0, NEAR - 1, unroll=unroll)
        def _(index):
            action(index + (index >= MIDDLE).astype(I32))

    for_neighbours(lambda slot: neighbour_copy(cells, place, cell_send, cell_recv, slot).start())

    def filter_to_field(level, own):
        out = along_y(own, FY, level)
        for b in range(8):
            high_field[8 * level : 8 * level + 8, 128 * b : 128 * b + 128] = out[8 * b : 8 * b + 8]

    for level in range(LEV):
        filter_to_field(level, grid[level])

    def both(slot, row):
        return jnp.concatenate([place[slot, row : row + 1, :], place[slot, row + 1 : row + 2, :]], axis=1)

    own_rows = both(MIDDLE, 2)
    row_number = iota((128, 256), 0).astype(F32)
    for block in range(8):
        hit = (row_number + float(128 * block)) == own_rows
        onehot_rows[128 * block : 128 * block + 128, :] = hit.astype(BF16)
    own_columns = both(MIDDLE, 0)
    own_column = jnp.broadcast_to(own_columns, (8, 256)) == iota((8, 256), 0).astype(F32)
    own_mask = jnp.broadcast_to(own_column[None], (LEV, 8, 256)).reshape(LEV * 8, 256)

    def sample():
        product = dot(stacked(high_field[...]), onehot_rows[...])
        product = product[:128] + product[128:]
        return jnp.sum(jnp.where(own_column[None], product.reshape(LEV, 8, 256), 0.0), axis=1)

    def apply_model(values):
        total = jnp.zeros((LEV, 256), F32)
        for k in range(LEV):
            total = total + model[k] * jnp.broadcast_to(values[k : k + 1], (LEV, 256))
        return total

    z0 = sample()
    q1 = apply_model(z0) - (extra[0:16, :] + extra[16:32, :])
    queue_a[...] = q1
    recv_a[MIDDLE] = q1
    for_neighbours(lambda slot: neighbour_copy(queue_a, recv_a, qa_send, qa_recv, slot).start())

    lane_number = iota((256, 128), 1).astype(F32)

    def build_onehot(slot):
        base = 256 * slot if isinstance(slot, int) else pl.multiple_of(256 * slot, 256)
        rows = place[slot]
        turned = jnp.transpose(jnp.concatenate([rows] + [jnp.zeros((8, 128), F32)] * 15, axis=0))
        rows_of = jnp.concatenate([turned[:, 2:3], turned[:, 3:4]], axis=0)
        rows_of = jnp.broadcast_to(rows_of, (256, 128))
        for block in range(8):
            hit = (lane_number + float(128 * block)) == rows_of
            onehot[pl.ds(base, 256), 128 * block : 128 * block + 128] = hit.astype(BF16)

        columns_of = both(slot, 0)
        wraps = slot == NEAR - 1
        first = jnp.where(wraps, 0, 8 * slot).astype(F32)
        hit = (row_number == columns_of + first).astype(BF16)
        product = dot(stacked(autocov[jnp.where(wraps, 1, 0)]), hit)
        near_x[slot] = product[:128] + product[128:]

    build_onehot(MIDDLE)

    def to_grid(pair, first, count, then):
        for quarter in range(4):
            total = dot(pair, onehot[first : first + count, 256 * quarter : 256 * quarter + 256])
            total = total[0:128] + total[128:256]
            for half in range(2):
                at = 16 * quarter + 8 * half
                grid[:, at : at + 8, :] = total[:, 128 * half : 128 * half + 128].reshape(LEV, 8, 128)
        for level in range(LEV):
            then(level, along_y(grid[level], BY, level))

    def own_adjoint(index, values):
        def keep(level, out):
            adjoint[index, level] = out

        to_grid(stacked(jnp.where(own_mask, spread_levels(values), 0.0)), 256 * MIDDLE, 256, keep)

    own_adjoint(0, q1)

    def arrive_cells(slot):
        neighbour_copy(cells, place, cell_send, cell_recv, slot).wait_recv()
        build_onehot(slot)

    for_neighbours(arrive_cells)

    def covary(source, target, send_sem, recv_sem):
        def add(slot):
            lanes = pl.ds(pl.multiple_of(256 * slot, 256), 256)
            spread_q[:, lanes] = stacked(near_x[slot] * spread_levels(target[slot]))

        add(MIDDLE)

        def arrived(slot):
            neighbour_copy(source, target, send_sem, recv_sem, slot).wait_recv()
            add(slot)

        for_neighbours(arrived)
        to_grid(spread_q[...], 0, REACH, filter_to_field)
        return sample()

    t1 = covary(queue_a, recv_a, qa_send, qa_recv)
    s0 = -(z0 + t1)
    q2 = apply_model(s0)
    queue_b[...] = q2
    recv_b[MIDDLE] = q2
    for_neighbours(lambda slot: neighbour_copy(queue_b, recv_b, qb_send, qb_recv, slot).start())
    own_adjoint(1, q2)
    c0c0 = jnp.sum(jnp.sum(c0_ref[...] * c0_ref[...], axis=0))
    t2 = covary(queue_b, recv_b, qb_send, qb_recv)
    u = apply_model(t2)

    lane = iota((1, 128), 1)
    row = jnp.zeros((1, 128), F32)
    for k, value in enumerate(
        (c0c0, jnp.sum(z0 * q1), jnp.sum(q1 * t1), jnp.sum(s0 * q2), jnp.sum(t2 * q2), jnp.sum(t2 * u))
    ):
        row = jnp.where(lane == k, value, row)
    part[...] = row
    total = exchange(part, sums, 1, lambda index: pl.ds(0, 1), sum_send, sum_recv)
    own_adjoint(2, u)
    total.wait_recv()
    summed = jnp.sum(sums[...], axis=0, keepdims=True)
    c0c0, z0q1, q1t1, s0q2, q2t2, t2u = [summed[:, k : k + 1] for k in range(6)]
    norm0 = c0c0 + 2.0 * z0q1 + q1t1
    alpha0 = norm0 / (norm0 + s0q2)
    keep = 1.0 - alpha0
    norm1 = keep * keep * norm0 - 2.0 * alpha0 * keep * s0q2 + alpha0 * alpha0 * q2t2
    beta0 = norm1 / norm0
    gain = keep + beta0
    curvature = gain * gain * s0q2 - 2.0 * gain * alpha0 * q2t2 + alpha0 * alpha0 * t2u
    alpha1 = norm1 / (norm1 + beta0 * beta0 * norm0 + curvature)
    coef_c = alpha0 + alpha1 * gain
    coef_r = (1.0 - alpha1) * keep - alpha1 * beta0
    control_2 = alpha0 * alpha1
    residual_2 = (1.0 - alpha1) * alpha0 + alpha1 * gain
    residual_u = -alpha1 * alpha0

    @pl.loop(0, 8)
    def _(block):
        at = pl.ds(pl.multiple_of(8 * block, 8), 8)
        first, second = [], []
        for level in range(LEV):
            one, two, three = [adjoint[k, level, at, :] for k in range(3)]
            first.append(coef_c * one + control_2 * two)
            second.append(coef_r * one + residual_2 * two + residual_u * three)
        first, second = swap_groups(first), swap_groups(second)
        for j in range(16):
            at = pl.ds(pl.multiple_of(256 * block + 16 * j, 16), 16)
            send_f[at, :] = jnp.concatenate([first[j], second[j]], axis=0).astype(BF16)

    final = exchange(send_f, recv_f, 16, tile_of, final_send, final_recv)
    final.wait_recv()

    for block in range(8):
        arrived = recv_f[256 * block : 256 * block + 256, :].astype(F32).reshape(16, 2, 8, 128)
        for index in range(2):
            turned = jnp.transpose(arrived[:, index].reshape(128, 128))
            adjoint[index, :, 8 * block : 8 * block + 8, :] = turned.reshape(LEV, 8, 128)

    for level in range(LEV):
        for index, (out_ref, coef) in enumerate(((control_ref, 1.0 - coef_c), (residual_ref, -coef_r))):
            out = along_x(adjoint[index, level], BX, level)
            for b in range(8):
                lanes = slice(128 * b, 128 * b + 128)
                out_ref[level, :, lanes] = coef * c0_ref[level, :, lanes] - out[8 * b : 8 * b + 8]

    dense.wait_send()
    total.wait_send()
    final.wait_send()

    def sent(slot):
        neighbour_copy(cells, place, cell_send, cell_recv, slot).wait_send()
        neighbour_copy(queue_a, recv_a, qa_send, qa_recv, slot).wait_send()
        neighbour_copy(queue_b, recv_b, qb_send, qb_recv, slot).wait_send()

    for_neighbours(sent)


def per_device(
    control_init, kernel_x, kernel_y, obs_weight, jacobian, innovation, obs_dest, obs_cell
):
    vmem = pl.BlockSpec(memory_space=pltpu.VMEM)
    anywhere = pl.BlockSpec(memory_space=pl.ANY)
    shape = jax.ShapeDtypeStruct(control_init.shape, F32)
    dma = pltpu.SemaphoreType.DMA
    return pl.pallas_call(
        kernel,
        out_shape=(shape, shape),
        in_specs=[anywhere] * 8,
        out_specs=(vmem, vmem),
        scratch_shapes=[
            pltpu.VMEM((LEV, 8, 1024), F32),
            pltpu.VMEM((LEV, TAPS), F32),
            pltpu.VMEM((LEV, TAPS), F32),
            pltpu.SMEM((CH,), F32),
            pltpu.VMEM((CH, LEV, 128), BF16),
            pltpu.VMEM((CH, 128), BF16),
            pltpu.VMEM((1, 128), I32),
            pltpu.VMEM((1, 128), I32),
            pltpu.VMEM((CH, 128), F32),
            pltpu.VMEM((4, LEV, 128), F32),
            pltpu.VMEM((4, LEV, 256, 256), BF16),
            pltpu.VMEM((8, LEV, 8, 128), F32),
            pltpu.VMEM((1024, 128), F32),
            pltpu.VMEM((2048, 128), BF16),
            pltpu.VMEM((2048, 128), BF16),
            pltpu.VMEM((2048, 128), F32),
            pltpu.VMEM((LEV, LEV, 256), F32),
            pltpu.VMEM((40, 256), F32),
            pltpu.VMEM((REACH, 1024), BF16),
            pltpu.VMEM((1024, 256), BF16),
            pltpu.VMEM((2, 128, 128), F32),
            pltpu.VMEM((NEAR, 128, 256), F32),
            pltpu.VMEM((NEAR, 8, 128), F32),
            pltpu.VMEM((8, 128), F32),
            pltpu.VMEM((LEV, 256), F32),
            pltpu.VMEM((LEV, 256), F32),
            pltpu.VMEM((NEAR, LEV, 256), F32),
            pltpu.VMEM((NEAR, LEV, 256), F32),
            pltpu.VMEM((256, REACH), BF16),
            pltpu.VMEM((LEV, 64, 128), F32),
            pltpu.VMEM((128, 1024), F32),
            pltpu.VMEM((3, LEV, 64, 128), F32),
            pltpu.VMEM((1, 128), F32),
            pltpu.VMEM((ND, 128), F32),
            pltpu.VMEM((2048, 128), BF16),
            pltpu.VMEM((2048, 128), BF16),
            dma((8,)),
            dma, dma,
            dma((NEAR,)), dma((NEAR,)),
            dma((NEAR,)), dma((NEAR,)), dma((NEAR,)), dma((NEAR,)),
            dma, dma, dma, dma,
        ],
        compiler_params=pltpu.CompilerParams(
            collective_id=0, has_side_effects=True, vmem_limit_bytes=60 * 1024 * 1024
        ),
    )(
        control_init,
        kernel_x,
        kernel_y,
        obs_weight,
        jnp.transpose(jacobian, (2, 1, 0)),
        jnp.transpose(innovation),
        jnp.transpose(obs_dest),
        obs_cell.reshape(1, -1),
    )


def solution(mesh):
    in_specs = (
        P(None, ("px", "py"), None),
        P(),
        P(),
        P(),
        P(("px", "py"), None, None),
        P(("px", "py"), None),
        P(("px", "py"), None),
        P(("px", "py")),
    )
    out_specs = (P(None, ("px", "py"), None), P(None, ("px", "py"), None))
    return jax.shard_map(
        per_device, mesh=mesh, in_specs=in_specs, out_specs=out_specs, check_vma=False
    )
```

time: 145 us -> 76.7 us (0.53)
  Pallas kernels: 137 us -> 72.1 us
  local copies, waits for them, and re-layouts: 6.9 us -> 3.77 us
    pallas_call x1, Pallas kernels: 137 us -> 72.1 us  [per_device(): pl.pallas_call(kernel, out_shape=(shape, shape), in_specs=[anywhere] * 8,...]
    unnamed x16 -> x2, local copies, waits for them, and re-layouts: 6.9 us -> 3.77 us
where the time goes in v2:
time: 76.7 us; the launch traced here: 76.5 us
  Pallas kernels  72.1 us (94%)
  local copies, waits for them, and re-layouts  3.77 us (5%)
    pallas_call x1, Pallas kernels, per_device(): pl.pallas_call(kernel, out_shape=(shape, shape), in_specs=[anywhere] * 8,...  72.1 us
    unnamed x2, local copies, waits for them, and re-layouts  3.77 us

profile of v2, /device:TPU:1, one launch (start us, length us, event | category | flops | bytes accessed | tf_op | source)
XLA Modules:
  0.0 76.5 jit_solution(13755058633519597538)
XLA Ops:
  0.6 72.1 %shard_map.95 = (f32[16,8,1024]{2,1,0:T(8,128)}, f32[16,8,1024]{2,1,0:T(8,128)}) custom-call(f32[16,8,1024]{2,1,0:T(8,128)} %c0_hbm.1, f32[16,64]{1,0:T(8,128)} %kx_hbm.1, f32[16,64]{1,0:T(8,128)} %ky_hbm.1, f32[431]{0:T(512)} %w_hbm.1, bf16[431,16,128]{2,1,0:T(8,128)(2,1)} %bitcast.4, bf16[431,128]{1,0:T(8,128)(2,1)} %bitcast.5, s32[1,128]{1,0:T(1,128)} %bitcast.6, ...), custom_call_target="tpu_custom_call" | custom-call | tf_op jit(solution)/shard_map/pallas_call | solution.py:473
  72.8 1.9 %copy.12 = f32[16,8,1024]{2,1,0:T(8,128)} copy(f32[16,8,1024]{2,1,0:T(8,128)} %get-tuple-element.4) | data formatting | bytes 1048576
  74.6 1.9 %copy.13 = f32[16,8,1024]{2,1,0:T(8,128)} copy(f32[16,8,1024]{2,1,0:T(8,128)} %get-tuple-element.5) | data formatting | bytes 1048576

commit v3 on v2

--- a/solution.py
+++ b/solution.py
@@ -61,11 +61,11 @@
     c0_hbm, kx_hbm, ky_hbm, w_hbm, jac_hbm, innov_hbm, dest_hbm, cell_hbm,
     control_ref, residual_ref,
     c0_ref, kx_ref, ky_ref, w_ref, jac, innov, dest_ref, cell_ref,
-    innov_wide, line, table, mixed, tile_m, send_g, recv_g, wide,
-    model, extra, onehot, onehot_rows, autocov, near_x, place, cells, queue_a, queue_b,
-    recv_a, recv_b, spread_q, grid, high_field, adjoint, part, sums, send_f, recv_f,
-    load_sem, dense_send, dense_recv, cell_send, cell_recv,
-    qa_send, qa_recv, qb_send, qb_recv, sum_send, sum_recv, final_send, final_recv,
+    innov_wide, line, table, mixed, tile_m, send_g, recv_g, wide, send_m, recv_m,
+    model_low, model_high, extra, onehot, onehot_rows, autocov, near_x, place, cells, queue_a, queue_b,
+    recv_a, recv_b, spread_q, grid, high_field, adjoint, field, send_u, recv_u, send_f, recv_f,
+    entered, load_sem, model_send, model_recv, dense_send, dense_recv, cell_send, cell_recv,
+    qa_send, qa_recv, qb_send, qb_recv, early_send, early_recv, final_send, final_recv,
 ):
     my_x, my_y = lax.axis_index("px"), lax.axis_index("py")
     me = my_x * NPY + my_y
@@ -87,10 +87,13 @@
 
     barrier = pltpu.get_barrier_semaphore()
 
-    @pl.loop(1, ND)
-    def _(step):
+    for step in range(1, NPY):
         pl.semaphore_signal(
-            barrier, inc=1, device_id=device((me + step) & (ND - 1)), device_id_type=MESH
+            barrier, inc=1, device_id=(my_x, (my_y + step) & (NPY - 1)), device_id_type=MESH
+        )
+    for step in range(1, NPX):
+        pl.semaphore_signal(
+            barrier, inc=1, device_id=((my_x + step) & (NPX - 1), my_y), device_id_type=MESH
         )
 
     loads[1].wait()
@@ -148,75 +151,38 @@
         for b in range(8):
             mixed[b, level] = out[8 * b : 8 * b + 8]
 
-    for load in loads[3:]:
-        load.wait()
-    innov_wide[...] = innov[...].astype(F32)
-
-    def one_channel(channel, carry):
-        values = jac[channel].astype(F32)
-        scaled = values * w_ref[channel]
-        matrix, rhs = carry
-        matrix = tuple(
-            m + scaled * jnp.broadcast_to(values[k : k + 1], (LEV, 128)) for k, m in enumerate(matrix)
-        )
-        return matrix, rhs + scaled * jnp.broadcast_to(innov_wide[pl.ds(channel, 1), :], (LEV, 128))
-
-    def some_channels(index, carry):
-        for k in range(8):
-            carry = one_channel(8 * index + k, carry)
-        return carry
-
-    zero = jnp.zeros((LEV, 128), F32)
-    carry = lax.fori_loop(0, CH // 8, some_channels, ((zero,) * LEV, zero))
-    for channel in range(CH // 8 * 8, CH):
-        carry = one_channel(channel, carry)
-    matrix, rhs = carry
-
+    loads[6].wait()
+    loads[7].wait()
     cell = cell_ref[...]
-    rhs_high, rhs_low = split(rhs)
-    codes = jnp.concatenate([(cell >> 10) + 1, (cell & 1023) >> 3, cell & 7, jnp.zeros((93, 128), I32)], axis=0)
-    pack = jnp.concatenate(
-        [m.astype(BF16) for m in matrix] + [rhs_high, rhs_low, codes.astype(F32).astype(BF16)], axis=0
-    )
+    codes = jnp.concatenate([(cell >> 10) + 1, (cell & 1023) >> 3, cell & 7, jnp.zeros((125, 128), I32)], axis=0)
     dest = jnp.broadcast_to(dest_ref[...], (128, 128))
     dest_t = jnp.transpose(dest.astype(F32))
     earlier = (dest.astype(F32) == dest_t) & (iota((128, 128), 0) < iota((128, 128), 1))
     rank = jnp.sum(earlier.astype(F32), axis=0, keepdims=True)
     named = iota((128, 128), 0) == dest
     chosen = jnp.concatenate([(named & (rank == float(k))).astype(BF16) for k in range(2)], axis=0)
-    packed = dot(chosen, pack, NT)
+    packed = dot(chosen, codes.astype(F32).astype(BF16), NT)
     for k in range(2):
-        for i in range(3):
-            tile_m[pl.ds(3 * k + i, 128, stride=8), :] = packed[128 * k : 128 * k + 128, 128 * i : 128 * i + 128]
-    for i in range(6, 8):
+        tile_m[pl.ds(k, 128, stride=8), :] = packed[128 * k : 128 * k + 128]
+    for i in range(2, 8):
         tile_m[pl.ds(i, 128, stride=8), :] = jnp.zeros((128, 128), F32)
 
-    @pl.loop(0, 8)
-    def _(block):
-        tiles = swap_groups([mixed[block, level] for level in range(LEV)])
-        for j in range(16):
-            lower = tile_m[pl.ds(pl.multiple_of(128 * block + 8 * j, 8), 8), :]
-            at = pl.ds(pl.multiple_of(256 * block + 16 * j, 16), 16)
-            send_g[at, :] = jnp.concatenate([tiles[j], lower], axis=0).astype(BF16)
-
-    pl.semaphore_wait(barrier, ND - 1)
-
-    def exchange(source, target, rows, source_of, send_sem, recv_sem):
-        mine = pl.ds(pl.multiple_of(me * rows, rows), rows)
-
-        @pl.loop(1, ND)
-        def _(step):
-            other = (me + step) & (ND - 1)
-            pltpu.make_async_remote_copy(
-                src_ref=source.at[source_of(other)],
-                dst_ref=target.at[mine],
-                send_sem=send_sem,
-                recv_sem=recv_sem,
-                device_id=device(other),
-                device_id_type=MESH,
-            ).start()
-
-        target[mine, :] = source[source_of(me), :]
+    pl.semaphore_wait(barrier, NPX + NPY - 2)
+    for step in range(1, NPX):
+        pl.semaphore_signal(
+            entered, inc=1, device_id=((my_x + step) & (NPX - 1), my_y), device_id_type=MESH
+        )
+    def send_one(source, target, rows, other, source_rows, send_sem, recv_sem):
+        pltpu.make_async_remote_copy(
+            src_ref=source.at[source_rows],
+            dst_ref=target.at[rows],
+            send_sem=send_sem,
+            recv_sem=recv_sem,
+            device_id=device(other),
+            device_id_type=MESH,
+        ).start()
+
+    def all_sent(target, rows, send_sem, recv_sem):
         whole = pl.ds(0, (ND - 1) * rows)
         return pltpu.make_async_remote_copy(
             src_ref=target.at[whole],
@@ -227,10 +193,83 @@
             device_id_type=MESH,
         )
 
-    def tile_of(index):
-        return pl.ds(pl.multiple_of(index * 16, 16), 16)
-
-    dense = exchange(send_g, recv_g, 16, tile_of, dense_send, dense_recv)
+    def rows_of(index, stride, count):
+        return pl.ds(pl.multiple_of(index * stride, stride), count)
+
+    def exchange(source, target, stride, count, send_sem, recv_sem):
+        mine = rows_of(me, stride, count)
+
+        @pl.loop(1, ND)
+        def _(step):
+            other = (me + step) & (ND - 1)
+            send_one(source, target, mine, other, rows_of(other, stride, count), send_sem, recv_sem)
+
+        target[mine, :] = source[mine, :]
+        return all_sent(target, count, send_sem, recv_sem)
+
+    def store_tiles(tiles, source, turn):
+        block = (my_x + turn) & (NPX - 1)
+        for j, tile in enumerate(tiles(block)):
+            source[pl.ds(pl.multiple_of(256 * block + 16 * j, 16), 16), :] = tile.astype(BF16)
+
+    def send_tiles(source, target, rows, turn, send_sem, recv_sem):
+        mine = rows_of(me, 16, rows)
+        block = (my_x + turn) & (NPX - 1)
+        for j in range(1 if turn == 0 else 0, NPY):
+            other = block * NPY + ((my_y + j) & (NPY - 1))
+            send_one(source, target, mine, other, rows_of(other, 16, rows), send_sem, recv_sem)
+
+    def keep_own(source, target, rows):
+        mine = rows_of(me, 16, rows)
+        target[mine, :] = source[mine, :]
+
+    def first_tiles(block):
+        tiles = swap_groups([mixed[block, level] for level in range(LEV)])
+        lower = [tile_m[pl.ds(pl.multiple_of(128 * block + 8 * j, 8), 8), :] for j in range(16)]
+        return [jnp.concatenate([tiles[j], lower[j]], axis=0) for j in range(16)]
+
+    for turn in range(NPX):
+        store_tiles(first_tiles, send_g, turn)
+    send_tiles(send_g, recv_g, 16, 0, dense_send, dense_recv)
+    pl.semaphore_wait(entered, NPX - 1)
+    for turn in range(1, NPX):
+        send_tiles(send_g, recv_g, 16, turn, dense_send, dense_recv)
+    keep_own(send_g, recv_g, 16)
+    dense = all_sent(recv_g, 16, dense_send, dense_recv)
+
+    for load in loads[3:6]:
+        load.wait()
+    innov_wide[...] = innov[...].astype(F32)
+
+    def one_channel(channel, carry):
+        values = jac[channel].astype(F32)
+        scaled = values * w_ref[channel]
+        low, high, rhs = carry
+        rows = [jnp.broadcast_to(values[k : k + 1], (8, 128)) for k in range(LEV)]
+        low = tuple(m + scaled[0:8] * rows[k] for k, m in enumerate(low))
+        high = tuple(m + scaled[8:16] * rows[8 + k] for k, m in enumerate(high))
+        return low, high, rhs + scaled * jnp.broadcast_to(innov_wide[pl.ds(channel, 1), :], (LEV, 128))
+
+    def some_channels(index, carry):
+        for k in range(8):
+            carry = one_channel(8 * index + k, carry)
+        return carry
+
+    zero = jnp.zeros((8, 128), F32)
+    carry = lax.fori_loop(
+        0, CH // 8, some_channels, ((zero,) * LEV, (zero,) * 8, jnp.zeros((LEV, 128), F32))
+    )
+    for channel in range(CH // 8 * 8, CH):
+        carry = one_channel(channel, carry)
+    low, high, rhs = carry
+    pack_high, pack_low = split(
+        jnp.concatenate(list(low) + list(high) + [rhs, jnp.zeros((48, 128), F32)], axis=0)
+    )
+    packed = dot(chosen, pack_high, NT) + dot(chosen, pack_low, NT)
+    for k in range(2):
+        for i in range(2):
+            send_m[pl.ds(2 * k + i, 128, stride=8), :] = packed[128 * k : 128 * k + 128, 128 * i : 128 * i + 128]
+    models = exchange(send_m, recv_m, 8, 4, model_send, model_recv)
 
     build_table(FY)
     build_table(BY)
@@ -251,20 +290,15 @@
     dense.wait_recv()
 
     for block in range(8):
-        values = recv_g[256 * block : 256 * block + 256, :].astype(F32)
-        wide[256 * block : 256 * block + 256, :] = values
-        turned = jnp.transpose(values.reshape(16, 16, 128)[:, 0:8].reshape(128, 128))
+        values = recv_g[256 * block : 256 * block + 256, :].astype(F32).reshape(16, 16, 128)
+        wide[128 * block : 128 * block + 128, :] = values[:, 8:16].reshape(128, 128)
+        turned = jnp.transpose(values[:, 0:8].reshape(128, 128))
         grid[:, 8 * block : 8 * block + 8, :] = turned.reshape(LEV, 8, 128)
 
     for k in range(2):
-        lanes = slice(128 * k, 128 * k + 128)
-        for i in range(2):
-            turned = jnp.transpose(wide[pl.ds(8 + 3 * k + i, 128, stride=16), :])
-            model[8 * i : 8 * i + 8, :, lanes] = turned.reshape(8, LEV, 128)
-        turned = jnp.transpose(wide[pl.ds(8 + 3 * k + 2, 128, stride=16), :])
-        extra[:, lanes] = turned[0:40]
-        cell_x = turned[32:33] - 1.0
-        cell_y = jnp.where(cell_x < 0.0, -1.0, 8.0 * turned[33:34] + turned[34:35])
+        turned = jnp.transpose(wide[pl.ds(k, 128, stride=8), :])
+        cell_x = turned[0:1] - 1.0
+        cell_y = jnp.where(cell_x < 0.0, -1.0, 8.0 * turned[1:2] + turned[2:3])
         cells[k : k + 1, :] = cell_x
         cells[2 + k : 3 + k, :] = cell_y
     cells[4:8, :] = jnp.zeros((4, 128), F32)
@@ -314,13 +348,27 @@
         return jnp.sum(jnp.where(own_column[None], product.reshape(LEV, 8, 256), 0.0), axis=1)
 
     def apply_model(values):
-        total = jnp.zeros((LEV, 256), F32)
+        lower, upper = values[0:8], values[8:16]
+        first = jnp.zeros((8, 256), F32)
+        second = jnp.zeros((8, 256), F32)
+        cross = []
         for k in range(LEV):
-            total = total + model[k] * jnp.broadcast_to(values[k : k + 1], (LEV, 256))
-        return total
+            first = first + model_low[k] * jnp.broadcast_to(values[k : k + 1], (8, 256))
+        for k in range(8):
+            second = second + model_high[k] * jnp.broadcast_to(upper[k : k + 1], (8, 256))
+            cross.append(jnp.sum(model_low[8 + k] * lower, axis=0, keepdims=True))
+        return jnp.concatenate([first, second + jnp.concatenate(cross, axis=0)], axis=0)
 
     z0 = sample()
-    q1 = apply_model(z0) - (extra[0:16, :] + extra[16:32, :])
+    models.wait_recv()
+    for k in range(2):
+        lanes = slice(128 * k, 128 * k + 128)
+        turned = jnp.transpose(recv_m[pl.ds(2 * k, 128, stride=8), :])
+        model_low[:, :, lanes] = turned.reshape(LEV, 8, 128)
+        turned = jnp.transpose(recv_m[pl.ds(2 * k + 1, 128, stride=8), :])
+        model_high[:, :, lanes] = turned[0:64].reshape(8, 8, 128)
+        extra[:, lanes] = turned[64:80]
+    q1 = apply_model(z0) - extra[...]
     queue_a[...] = q1
     recv_a[MIDDLE] = q1
     for_neighbours(lambda slot: neighbour_copy(queue_a, recv_a, qa_send, qa_recv, slot).start())
@@ -346,21 +394,25 @@
 
     build_onehot(MIDDLE)
 
-    def to_grid(pair, first, count, then):
-        for quarter in range(4):
-            total = dot(pair, onehot[first : first + count, 256 * quarter : 256 * quarter + 256])
-            total = total[0:128] + total[128:256]
-            for half in range(2):
-                at = 16 * quarter + 8 * half
-                grid[:, at : at + 8, :] = total[:, 128 * half : 128 * half + 128].reshape(LEV, 8, 128)
+    def from_grid(then):
         for level in range(LEV):
             then(level, along_y(grid[level], BY, level))
+
+    def to_grid(quarter, total):
+        total = total[0:128] + total[128:256]
+        for half in range(2):
+            at = 16 * quarter + 8 * half
+            grid[:, at : at + 8, :] = total[:, 128 * half : 128 * half + 128].reshape(LEV, 8, 128)
 
     def own_adjoint(index, values):
         def keep(level, out):
             adjoint[index, level] = out
 
-        to_grid(stacked(jnp.where(own_mask, spread_levels(values), 0.0)), 256 * MIDDLE, 256, keep)
+        pair = stacked(jnp.where(own_mask, spread_levels(values), 0.0))
+        for quarter in range(4):
+            hits = onehot[256 * MIDDLE : 256 * MIDDLE + 256, 256 * quarter : 256 * quarter + 256]
+            to_grid(quarter, dot(pair, hits))
+        from_grid(keep)
 
     own_adjoint(0, q1)
 
@@ -370,43 +422,82 @@
 
     for_neighbours(arrive_cells)
 
-    def covary(source, target, send_sem, recv_sem):
-        def add(slot):
-            lanes = pl.ds(pl.multiple_of(256 * slot, 256), 256)
-            spread_q[:, lanes] = stacked(near_x[slot] * spread_levels(target[slot]))
-
-        add(MIDDLE)
-
-        def arrived(slot):
-            neighbour_copy(source, target, send_sem, recv_sem, slot).wait_recv()
-            add(slot)
-
-        for_neighbours(arrived)
-        to_grid(spread_q[...], 0, REACH, filter_to_field)
+    groups = ((0, 4), (4, 9), (9, 13), (13, 17))
+
+    def covary(source, target, send_sem, recv_sem, beside):
+        for number, (first, last) in enumerate(groups):
+            for slot in range(first, last):
+                if slot != MIDDLE:
+                    neighbour_copy(source, target, send_sem, recv_sem, slot).wait_recv()
+                spread_q[:, 256 * slot : 256 * slot + 256] = stacked(near_x[slot] * spread_levels(target[slot]))
+            for quarter in range(4):
+                total = dot(
+                    spread_q[:, 256 * first : 256 * last],
+                    onehot[256 * first : 256 * last, 256 * quarter : 256 * quarter + 256],
+                )
+                if number:
+                    total = total + field[quarter]
+                if number == len(groups) - 1:
+                    to_grid(quarter, total)
+                else:
+                    field[quarter] = total
+            beside(number)
+        from_grid(filter_to_field)
         return sample()
 
-    t1 = covary(queue_a, recv_a, qa_send, qa_recv)
+    t1 = covary(queue_a, recv_a, qa_send, qa_recv, lambda number: None)
     s0 = -(z0 + t1)
     q2 = apply_model(s0)
     queue_b[...] = q2
     recv_b[MIDDLE] = q2
     for_neighbours(lambda slot: neighbour_copy(queue_b, recv_b, qb_send, qb_recv, slot).start())
     own_adjoint(1, q2)
+
+    def early_tiles(block):
+        at = pl.ds(pl.multiple_of(8 * block, 8), 8)
+        first, second = [
+            swap_groups([adjoint[k, level, at, :] for level in range(LEV)]) for k in range(2)
+        ]
+        return [jnp.concatenate([first[j], second[j]], axis=0) for j in range(16)]
+
+    def send_early(number):
+        for turn in (2 * number, 2 * number + 1):
+            store_tiles(early_tiles, send_f, turn)
+            send_tiles(send_f, recv_f, 16, turn, early_send, early_recv)
+
+    t2 = covary(queue_b, recv_b, qb_send, qb_recv, send_early)
+    keep_own(send_f, recv_f, 16)
+    early = all_sent(recv_f, 16, early_send, early_recv)
+    u = apply_model(t2)
+
+    own_adjoint(2, u)
     c0c0 = jnp.sum(jnp.sum(c0_ref[...] * c0_ref[...], axis=0))
-    t2 = covary(queue_b, recv_b, qb_send, qb_recv)
-    u = apply_model(t2)
-
     lane = iota((1, 128), 1)
     row = jnp.zeros((1, 128), F32)
     for k, value in enumerate(
         (c0c0, jnp.sum(z0 * q1), jnp.sum(q1 * t1), jnp.sum(s0 * q2), jnp.sum(t2 * q2), jnp.sum(t2 * u))
     ):
         row = jnp.where(lane == k, value, row)
-    part[...] = row
-    total = exchange(part, sums, 1, lambda index: pl.ds(0, 1), sum_send, sum_recv)
-    own_adjoint(2, u)
-    total.wait_recv()
-    summed = jnp.sum(sums[...], axis=0, keepdims=True)
+
+    for turn in range(NPX):
+        block = (my_x + turn) & (NPX - 1)
+        at = pl.ds(pl.multiple_of(8 * block, 8), 8)
+        for j, tile in enumerate(swap_groups([adjoint[2, level, at, :] for level in range(LEV)])):
+            send_u[pl.ds(pl.multiple_of(256 * block + 16 * j, 16), 8), :] = tile
+            send_u[pl.ds(256 * block + 16 * j + 8, 1), :] = row
+        send_tiles(send_u, recv_u, 9, turn, final_send, final_recv)
+    keep_own(send_u, recv_u, 9)
+    final = all_sent(recv_u, 9, final_send, final_recv)
+
+    early.wait_recv()
+    for block in range(8):
+        arrived = recv_f[256 * block : 256 * block + 256, :].astype(F32).reshape(16, 2, 8, 128)
+        for index in range(2):
+            turned = jnp.transpose(arrived[:, index].reshape(128, 128))
+            adjoint[index, :, 8 * block : 8 * block + 8, :] = turned.reshape(LEV, 8, 128)
+
+    final.wait_recv()
+    summed = jnp.sum(recv_u[pl.ds(8, ND, stride=16), :], axis=0, keepdims=True)
     c0c0, z0q1, q1t1, s0q2, q2t2, t2u = [summed[:, k : k + 1] for k in range(6)]
     norm0 = c0c0 + 2.0 * z0q1 + q1t1
     alpha0 = norm0 / (norm0 + s0q2)
@@ -422,37 +513,25 @@
     residual_2 = (1.0 - alpha1) * alpha0 + alpha1 * gain
     residual_u = -alpha1 * alpha0
 
-    @pl.loop(0, 8)
-    def _(block):
-        at = pl.ds(pl.multiple_of(8 * block, 8), 8)
-        first, second = [], []
-        for level in range(LEV):
-            one, two, three = [adjoint[k, level, at, :] for k in range(3)]
-            first.append(coef_c * one + control_2 * two)
-            second.append(coef_r * one + residual_2 * two + residual_u * three)
-        first, second = swap_groups(first), swap_groups(second)
-        for j in range(16):
-            at = pl.ds(pl.multiple_of(256 * block + 16 * j, 16), 16)
-            send_f[at, :] = jnp.concatenate([first[j], second[j]], axis=0).astype(BF16)
-
-    final = exchange(send_f, recv_f, 16, tile_of, final_send, final_recv)
-    final.wait_recv()
-
     for block in range(8):
-        arrived = recv_f[256 * block : 256 * block + 256, :].astype(F32).reshape(16, 2, 8, 128)
-        for index in range(2):
-            turned = jnp.transpose(arrived[:, index].reshape(128, 128))
-            adjoint[index, :, 8 * block : 8 * block + 8, :] = turned.reshape(LEV, 8, 128)
+        arrived = recv_u[256 * block : 256 * block + 256, :].reshape(16, 16, 128)[:, 0:8]
+        turned = jnp.transpose(arrived.reshape(128, 128))
+        adjoint[2, :, 8 * block : 8 * block + 8, :] = turned.reshape(LEV, 8, 128)
 
     for level in range(LEV):
-        for index, (out_ref, coef) in enumerate(((control_ref, 1.0 - coef_c), (residual_ref, -coef_r))):
-            out = along_x(adjoint[index, level], BX, level)
+        one, two, three = [adjoint[k, level] for k in range(3)]
+        for out_ref, coef, value in (
+            (control_ref, 1.0 - coef_c, coef_c * one + control_2 * two),
+            (residual_ref, -coef_r, coef_r * one + residual_2 * two + residual_u * three),
+        ):
+            out = along_x(value, BX, level)
             for b in range(8):
                 lanes = slice(128 * b, 128 * b + 128)
                 out_ref[level, :, lanes] = coef * c0_ref[level, :, lanes] - out[8 * b : 8 * b + 8]
 
     dense.wait_send()
-    total.wait_send()
+    models.wait_send()
+    early.wait_send()
     final.wait_send()
 
     def sent(slot):
@@ -491,9 +570,12 @@
             pltpu.VMEM((1024, 128), F32),
             pltpu.VMEM((2048, 128), BF16),
             pltpu.VMEM((2048, 128), BF16),
-            pltpu.VMEM((2048, 128), F32),
-            pltpu.VMEM((LEV, LEV, 256), F32),
-            pltpu.VMEM((40, 256), F32),
+            pltpu.VMEM((1024, 128), F32),
+            pltpu.VMEM((1024, 128), F32),
+            pltpu.VMEM((1024, 128), F32),
+            pltpu.VMEM((LEV, 8, 256), F32),
+            pltpu.VMEM((8, 8, 256), F32),
+            pltpu.VMEM((LEV, 256), F32),
             pltpu.VMEM((REACH, 1024), BF16),
             pltpu.VMEM((1024, 256), BF16),
             pltpu.VMEM((2, 128, 128), F32),
@@ -508,12 +590,14 @@
             pltpu.VMEM((LEV, 64, 128), F32),
             pltpu.VMEM((128, 1024), F32),
             pltpu.VMEM((3, LEV, 64, 128), F32),
-            pltpu.VMEM((1, 128), F32),
-            pltpu.VMEM((ND, 128), F32),
+            pltpu.VMEM((4, 256, 256), F32),
+            pltpu.VMEM((2048, 128), F32),
+            pltpu.VMEM((2048, 128), F32),
             pltpu.VMEM((2048, 128), BF16),
             pltpu.VMEM((2048, 128), BF16),
+            pltpu.SemaphoreType.REGULAR,
             dma((8,)),
-            dma, dma,
+            dma, dma, dma, dma,
             dma((NEAR,)), dma((NEAR,)),
             dma((NEAR,)), dma((NEAR,)), dma((NEAR,)), dma((NEAR,)),
             dma, dma, dma, dma,

time: 76.7 us -> 65.9 us (0.86)
  Pallas kernels: 72.1 us -> 61.3 us
    pallas_call x1, Pallas kernels: 72.1 us -> 61.3 us  [per_device(): pl.pallas_call(kernel, out_shape=(shape, shape), in_specs=[anywhere] * 8,...]
where the time goes in v3:
time: 65.9 us; the launch traced here: 65.7 us
  Pallas kernels  61.3 us (93%)
  local copies, waits for them, and re-layouts  3.77 us (6%)
    pallas_call x1, Pallas kernels, per_device(): pl.pallas_call(kernel, out_shape=(shape, shape), in_specs=[anywhere] * 8,...  61.3 us
    unnamed x2, local copies, waits for them, and re-layouts  3.77 us

profile of v3, /device:TPU:1, one launch (start us, length us, event | category | flops | bytes accessed | tf_op | source)
XLA Modules:
  0.0 65.7 jit_solution(17583776513227596478)
XLA Ops:
  0.6 61.3 %shard_map.95 = (f32[16,8,1024]{2,1,0:T(8,128)}, f32[16,8,1024]{2,1,0:T(8,128)}) custom-call(f32[16,8,1024]{2,1,0:T(8,128)} %c0_hbm.1, f32[16,64]{1,0:T(8,128)} %kx_hbm.1, f32[16,64]{1,0:T(8,128)} %ky_hbm.1, f32[431]{0:T(512)} %w_hbm.1, bf16[431,16,128]{2,1,0:T(8,128)(2,1)} %bitcast.4, bf16[431,128]{1,0:T(8,128)(2,1)} %bitcast.5, s32[1,128]{1,0:T(1,128)} %bitcast.6, ...), custom_call_target="tpu_custom_call" | custom-call | tf_op jit(solution)/shard_map/pallas_call | solution.py:552
  61.9 1.9 %copy.12 = f32[16,8,1024]{2,1,0:T(8,128)} copy(f32[16,8,1024]{2,1,0:T(8,128)} %get-tuple-element.4) | data formatting | bytes 1048576
  63.8 1.9 %copy.13 = f32[16,8,1024]{2,1,0:T(8,128)} copy(f32[16,8,1024]{2,1,0:T(8,128)} %get-tuple-element.5) | data formatting | bytes 1048576

commit v4 on v3

--- a/solution.py
+++ b/solution.py
@@ -59,12 +59,12 @@
 
 def kernel(
     c0_hbm, kx_hbm, ky_hbm, w_hbm, jac_hbm, innov_hbm, dest_hbm, cell_hbm,
-    control_ref, residual_ref,
+    control_hbm, residual_hbm,
     c0_ref, kx_ref, ky_ref, w_ref, jac, innov, dest_ref, cell_ref,
     innov_wide, line, table, mixed, tile_m, send_g, recv_g, wide, send_m, recv_m,
     model_low, model_high, extra, onehot, onehot_rows, autocov, near_x, place, cells, queue_a, queue_b,
-    recv_a, recv_b, spread_q, grid, high_field, adjoint, field, send_u, recv_u, send_f, recv_f,
-    entered, load_sem, model_send, model_recv, dense_send, dense_recv, cell_send, cell_recv,
+    recv_a, recv_b, spread_q, grid, high_field, adjoint, field, change, send_u, recv_u, send_f, recv_f,
+    entered, load_sem, store_sem, model_send, model_recv, dense_send, dense_recv, cell_send, cell_recv,
     qa_send, qa_recv, qb_send, qb_recv, early_send, early_recv, final_send, final_recv,
 ):
     my_x, my_y = lax.axis_index("px"), lax.axis_index("py")
@@ -196,17 +196,6 @@
     def rows_of(index, stride, count):
         return pl.ds(pl.multiple_of(index * stride, stride), count)
 
-    def exchange(source, target, stride, count, send_sem, recv_sem):
-        mine = rows_of(me, stride, count)
-
-        @pl.loop(1, ND)
-        def _(step):
-            other = (me + step) & (ND - 1)
-            send_one(source, target, mine, other, rows_of(other, stride, count), send_sem, recv_sem)
-
-        target[mine, :] = source[mine, :]
-        return all_sent(target, count, send_sem, recv_sem)
-
     def store_tiles(tiles, source, turn):
         block = (my_x + turn) & (NPX - 1)
         for j, tile in enumerate(tiles(block)):
@@ -269,7 +258,18 @@
     for k in range(2):
         for i in range(2):
             send_m[pl.ds(2 * k + i, 128, stride=8), :] = packed[128 * k : 128 * k + 128, 128 * i : 128 * i + 128]
-    models = exchange(send_m, recv_m, 8, 4, model_send, model_recv)
+    own_rows = rows_of(me, 8, 4)
+
+    def send_model(step):
+        other = (me + step) & (ND - 1)
+        send_one(send_m, recv_m, own_rows, other, rows_of(other, 8, 4), model_send, model_recv)
+
+    @pl.loop(1, ND)
+    def _(step):
+        send_model(step)
+
+    recv_m[own_rows, :] = send_m[own_rows, :]
+    models = all_sent(recv_m, 4, model_send, model_recv)
 
     build_table(FY)
     build_table(BY)
@@ -462,22 +462,28 @@
 
     def send_early(number):
         for turn in (2 * number, 2 * number + 1):
-            store_tiles(early_tiles, send_f, turn)
             send_tiles(send_f, recv_f, 16, turn, early_send, early_recv)
 
+    for turn in range(NPX):
+        store_tiles(early_tiles, send_f, turn)
+    keep_own(send_f, recv_f, 16)
+    lane = iota((1, 128), 1)
+
+    def place_sums(row, first, values):
+        for k, value in enumerate(values):
+            row = jnp.where(lane == first + k, value, row)
+        return row
+
+    c0c0 = jnp.sum(jnp.sum(c0_ref[...] * c0_ref[...], axis=0))
+    row = place_sums(
+        jnp.zeros((1, 128), F32), 0, (c0c0, jnp.sum(z0 * q1), jnp.sum(q1 * t1), jnp.sum(s0 * q2))
+    )
     t2 = covary(queue_b, recv_b, qb_send, qb_recv, send_early)
-    keep_own(send_f, recv_f, 16)
     early = all_sent(recv_f, 16, early_send, early_recv)
     u = apply_model(t2)
 
     own_adjoint(2, u)
-    c0c0 = jnp.sum(jnp.sum(c0_ref[...] * c0_ref[...], axis=0))
-    lane = iota((1, 128), 1)
-    row = jnp.zeros((1, 128), F32)
-    for k, value in enumerate(
-        (c0c0, jnp.sum(z0 * q1), jnp.sum(q1 * t1), jnp.sum(s0 * q2), jnp.sum(t2 * q2), jnp.sum(t2 * u))
-    ):
-        row = jnp.where(lane == k, value, row)
+    row = place_sums(row, 4, (jnp.sum(t2 * q2), jnp.sum(t2 * u)))
 
     for turn in range(NPX):
         block = (my_x + turn) & (NPX - 1)
@@ -520,14 +526,20 @@
 
     for level in range(LEV):
         one, two, three = [adjoint[k, level] for k in range(3)]
-        for out_ref, coef, value in (
-            (control_ref, 1.0 - coef_c, coef_c * one + control_2 * two),
-            (residual_ref, -coef_r, coef_r * one + residual_2 * two + residual_u * three),
+        for index, coef, value in (
+            (0, -coef_c, coef_c * one + control_2 * two),
+            (1, 1.0 - coef_r, coef_r * one + residual_2 * two + residual_u * three),
         ):
             out = along_x(value, BX, level)
             for b in range(8):
                 lanes = slice(128 * b, 128 * b + 128)
-                out_ref[level, :, lanes] = coef * c0_ref[level, :, lanes] - out[8 * b : 8 * b + 8]
+                change[index, level, :, lanes] = coef * c0_ref[level, :, lanes] - out[8 * b : 8 * b + 8]
+            pltpu.make_async_copy(
+                change.at[index, level], (control_hbm, residual_hbm)[index].at[level], store_sem.at[index]
+            ).start()
+
+    for index, target in enumerate((control_hbm, residual_hbm)):
+        pltpu.make_async_copy(change.at[index], target, store_sem.at[index]).wait()
 
     dense.wait_send()
     models.wait_send()
@@ -545,15 +557,14 @@
 def per_device(
     control_init, kernel_x, kernel_y, obs_weight, jacobian, innovation, obs_dest, obs_cell
 ):
-    vmem = pl.BlockSpec(memory_space=pltpu.VMEM)
     anywhere = pl.BlockSpec(memory_space=pl.ANY)
     shape = jax.ShapeDtypeStruct(control_init.shape, F32)
     dma = pltpu.SemaphoreType.DMA
-    return pl.pallas_call(
+    change, shifted = pl.pallas_call(
         kernel,
         out_shape=(shape, shape),
         in_specs=[anywhere] * 8,
-        out_specs=(vmem, vmem),
+        out_specs=(anywhere, anywhere),
         scratch_shapes=[
             pltpu.VMEM((LEV, 8, 1024), F32),
             pltpu.VMEM((LEV, TAPS), F32),
@@ -591,12 +602,13 @@
             pltpu.VMEM((128, 1024), F32),
             pltpu.VMEM((3, LEV, 64, 128), F32),
             pltpu.VMEM((4, 256, 256), F32),
+            pltpu.VMEM((2, LEV, 8, 1024), F32),
             pltpu.VMEM((2048, 128), F32),
             pltpu.VMEM((2048, 128), F32),
             pltpu.VMEM((2048, 128), BF16),
             pltpu.VMEM((2048, 128), BF16),
             pltpu.SemaphoreType.REGULAR,
-            dma((8,)),
+            dma((8,)), dma((2,)),
             dma, dma, dma, dma,
             dma((NEAR,)), dma((NEAR,)),
             dma((NEAR,)), dma((NEAR,)), dma((NEAR,)), dma((NEAR,)),
@@ -615,6 +627,7 @@
         jnp.transpose(obs_dest),
         obs_cell.reshape(1, -1),
     )
+    return control_init + change, shifted - control_init
 
 
 def solution(mesh):

time: 65.9 us -> 62.7 us (0.951)
  local copies, waits for them, and re-layouts: 3.77 us -> 0.01 us
  other arithmetic: 0 us -> 2.31 us
  Pallas kernels: 61.3 us -> 59.5 us
    unnamed x2, local copies, waits for them, and re-layouts: 3.77 us -> 0.01 us
    sub x0 -> x1, other arithmetic: none -> 2.31 us  [per_device(): return (control_init + change, shifted - control_init)]
    pallas_call x1, Pallas kernels: 61.3 us -> 59.5 us  [per_device(): pl.pallas_call(kernel, out_shape=(shape, shape), in_specs=[anywhere] * 8,...]
where the time goes in v4:
time: 62.7 us; the launch traced here: 62.5 us
  Pallas kernels  59.5 us (95%)
  other arithmetic  2.31 us (4%)
  between operations  0.66 us (1%)
    pallas_call x1, Pallas kernels, per_device(): pl.pallas_call(kernel, out_shape=(shape, shape), in_specs=[anywhere] * 8,...  59.5 us
    sub x1, other arithmetic, per_device(): return (control_init + change, shifted - control_init)  2.31 us

profile of v4, /device:TPU:1, one launch (start us, length us, event | category | flops | bytes accessed | tf_op | source)
XLA Modules:
  0.0 62.5 jit_solution(17309060007661809360)
XLA Ops:
  0.6 0.0 copy-start
  0.6 59.5 %shard_map.95 = (f32[16,8,1024]{2,1,0:T(8,128)}, f32[16,8,1024]{2,1,0:T(8,128)}) custom-call(f32[16,8,1024]{2,1,0:T(8,128)} %c0_hbm.1, f32[16,64]{1,0:T(8,128)} %kx_hbm.1, f32[16,64]{1,0:T(8,128)} %ky_hbm.1, f32[431]{0:T(512)} %w_hbm.1, bf16[431,16,128]{2,1,0:T(8,128)(2,1)} %bitcast.4, bf16[431,128]{1,0:T(8,128)(2,1)} %bitcast.5, s32[1,128]{1,0:T(1,128)} %bitcast.6, ...), custom_call_target="tpu_custom_call" | custom-call | tf_op jit(solution)/shard_map/pallas_call | solution.py:563
  60.2 0.0 copy-done
  60.2 2.3 %fusion = (f32[16,8,1024]{2,1,0:T(8,128)}, f32[16,8,1024]{2,1,0:T(8,128)}) fusion(f32[16,8,1024]{2,1,0:T(8,128)} %get-tuple-element.5, f32[16,8,1024]{2,1,0:T(8,128)S(1)} %copy-done, f32[16,8,1024]{2,1,0:T(8,128)} %get-tuple-element.4), kind=kLoop, calls=%fused_computation | loop fusion | flops 262144 | bytes 2621440 | tf_op jit(solution)/shard_map/sub | solution.py:630
Async XLA Ops:
  0.6 59.6 %copy-start = (f32[16,8,1024]{2,1,0:T(8,128)S(1)}, f32[16,8,1024]{2,1,0:T(8,128)}, u32[]{:S(2)}) copy-start(f32[16,8,1024]{2,1,0:T(8,128)} %c0_hbm.1) | copy-start | bytes 1572868

commit v5 on v4

--- a/solution.py
+++ b/solution.py
@@ -228,7 +228,7 @@
 
     for load in loads[3:6]:
         load.wait()
-    innov_wide[...] = innov[...].astype(F32)
+    innov_wide[0:CH, :] = innov[...].astype(F32)
 
     def one_channel(channel, carry):
         values = jac[channel].astype(F32)
@@ -272,20 +272,6 @@
     models = all_sent(recv_m, 4, model_send, model_recv)
 
     build_table(FY)
-    build_table(BY)
-    build_table(BX)
-
-    column = iota((8, 128), 1)
-    offset = iota((8, 128), 0)
-
-    @pl.loop(0, LEV, unroll=4)
-    def _(level):
-        taps = line[BX, pl.ds(level, 1), :]
-        cov = dot(jnp.broadcast_to(taps, (8, 128)), circulant(taps), NT, precision=HIGHEST)
-        ring = pltpu.roll(cov, 64, 1, stride=1, stride_axis=0)
-        at = pl.ds(pl.multiple_of(8 * level, 8), 8)
-        autocov[0, at, :] = jnp.where(column > offset, ring, 0.0)
-        autocov[1, at, :] = jnp.where(column < offset, ring, 0.0)
 
     dense.wait_recv()
 
@@ -372,6 +358,21 @@
     queue_a[...] = q1
     recv_a[MIDDLE] = q1
     for_neighbours(lambda slot: neighbour_copy(queue_a, recv_a, qa_send, qa_recv, slot).start())
+
+    build_table(BY)
+    build_table(BX)
+
+    column = iota((8, 128), 1)
+    offset = iota((8, 128), 0)
+
+    @pl.loop(0, LEV, unroll=4)
+    def _(level):
+        taps = line[BX, pl.ds(level, 1), :]
+        cov = dot(jnp.broadcast_to(taps, (8, 128)), circulant(taps), NT, precision=HIGHEST)
+        ring = pltpu.roll(cov, 64, 1, stride=1, stride_axis=0)
+        at = pl.ds(pl.multiple_of(8 * level, 8), 8)
+        autocov[0, at, :] = jnp.where(column > offset, ring, 0.0)
+        autocov[1, at, :] = jnp.where(column < offset, ring, 0.0)
 
     lane_number = iota((256, 128), 1).astype(F32)
 
@@ -574,7 +575,7 @@
             pltpu.VMEM((CH, 128), BF16),
             pltpu.VMEM((1, 128), I32),
             pltpu.VMEM((1, 128), I32),
-            pltpu.VMEM((CH, 128), F32),
+            pltpu.VMEM((CH + 1, 128), F32),
             pltpu.VMEM((4, LEV, 128), F32),
             pltpu.VMEM((4, LEV, 256, 256), BF16),
             pltpu.VMEM((8, LEV, 8, 128), F32),

time: 62.7 us -> 66.2 us (1.056)
  Pallas kernels: 59.5 us -> 63.1 us
    pallas_call x1, Pallas kernels: 59.5 us -> 63.1 us  [per_device(): pl.pallas_call(kernel, out_shape=(shape, shape), in_specs=[anywhere] * 8,...]
where the time goes in v5:
time: 66.2 us; the launch traced here: 66.1 us
  Pallas kernels  63.1 us (95%)
  other arithmetic  2.31 us (3%)
    pallas_call x1, Pallas kernels, per_device(): pl.pallas_call(kernel, out_shape=(shape, shape), in_specs=[anywhere] * 8,...  63.1 us
    sub x1, other arithmetic, per_device(): return (control_init + change, shifted - control_init)  2.31 us

profile of v5, /device:TPU:1, one launch (start us, length us, event | category | flops | bytes accessed | tf_op | source)
XLA Modules:
  0.0 66.1 jit_solution(16668990986668226099)
XLA Ops:
  0.6 0.0 copy-start
  0.6 63.1 %shard_map.95 = (f32[16,8,1024]{2,1,0:T(8,128)}, f32[16,8,1024]{2,1,0:T(8,128)}) custom-call(f32[16,8,1024]{2,1,0:T(8,128)} %c0_hbm.1, f32[16,64]{1,0:T(8,128)} %kx_hbm.1, f32[16,64]{1,0:T(8,128)} %ky_hbm.1, f32[431]{0:T(512)} %w_hbm.1, bf16[431,16,128]{2,1,0:T(8,128)(2,1)} %bitcast.4, bf16[431,128]{1,0:T(8,128)(2,1)} %bitcast.5, s32[1,128]{1,0:T(1,128)} %bitcast.6, ...), custom_call_target="tpu_custom_call" | custom-call | tf_op jit(solution)/shard_map/pallas_call | solution.py:564
  63.7 0.0 copy-done
  63.7 2.3 %fusion = (f32[16,8,1024]{2,1,0:T(8,128)}, f32[16,8,1024]{2,1,0:T(8,128)}) fusion(f32[16,8,1024]{2,1,0:T(8,128)} %get-tuple-element.5, f32[16,8,1024]{2,1,0:T(8,128)S(1)} %copy-done, f32[16,8,1024]{2,1,0:T(8,128)} %get-tuple-element.4), kind=kLoop, calls=%fused_computation | loop fusion | flops 262144 | bytes 2621440 | tf_op jit(solution)/shard_map/sub | solution.py:631
Async XLA Ops:
  0.6 63.1 %copy-start = (f32[16,8,1024]{2,1,0:T(8,128)S(1)}, f32[16,8,1024]{2,1,0:T(8,128)}, u32[]{:S(2)}) copy-start(f32[16,8,1024]{2,1,0:T(8,128)} %c0_hbm.1) | copy-start | bytes 1572868

commit v6 on v4

--- a/solution.py
+++ b/solution.py
@@ -414,13 +414,8 @@
             to_grid(quarter, dot(pair, hits))
         from_grid(keep)
 
-    own_adjoint(0, q1)
-
-    def arrive_cells(slot):
-        neighbour_copy(cells, place, cell_send, cell_recv, slot).wait_recv()
-        build_onehot(slot)
-
-    for_neighbours(arrive_cells)
+    for_neighbours(lambda slot: neighbour_copy(cells, place, cell_send, cell_recv, slot).wait_recv())
+    for_neighbours(build_onehot, unroll=2)
 
     groups = ((0, 4), (4, 9), (9, 13), (13, 17))
 
@@ -451,6 +446,7 @@
     queue_b[...] = q2
     recv_b[MIDDLE] = q2
     for_neighbours(lambda slot: neighbour_copy(queue_b, recv_b, qb_send, qb_recv, slot).start())
+    own_adjoint(0, q1)
     own_adjoint(1, q2)
 
     def early_tiles(block):

time: 62.7 us -> 62.9 us (level)
  no operation moved by 1% of the time
where the time goes in v6:
time: 62.9 us; the launch traced here: 62.8 us
  Pallas kernels  59.8 us (95%)
  other arithmetic  2.31 us (4%)
  between operations  0.66 us (1%)
    pallas_call x1, Pallas kernels, per_device(): pl.pallas_call(kernel, out_shape=(shape, shape), in_specs=[anywhere] * 8,...  59.8 us
    sub x1, other arithmetic, per_device(): return (control_init + change, shifted - control_init)  2.31 us

profile of v6, /device:TPU:1, one launch (start us, length us, event | category | flops | bytes accessed | tf_op | source)
XLA Modules:
  0.0 62.8 jit_solution(17493405173738066992)
XLA Ops:
  0.6 0.0 copy-start
  0.6 59.8 %shard_map.95 = (f32[16,8,1024]{2,1,0:T(8,128)}, f32[16,8,1024]{2,1,0:T(8,128)}) custom-call(f32[16,8,1024]{2,1,0:T(8,128)} %c0_hbm.1, f32[16,64]{1,0:T(8,128)} %kx_hbm.1, f32[16,64]{1,0:T(8,128)} %ky_hbm.1, f32[431]{0:T(512)} %w_hbm.1, bf16[431,16,128]{2,1,0:T(8,128)(2,1)} %bitcast.4, bf16[431,128]{1,0:T(8,128)(2,1)} %bitcast.5, s32[1,128]{1,0:T(1,128)} %bitcast.6, ...), custom_call_target="tpu_custom_call" | custom-call | tf_op jit(solution)/shard_map/pallas_call | solution.py:559
  60.4 0.0 copy-done
  60.5 2.3 %fusion = (f32[16,8,1024]{2,1,0:T(8,128)}, f32[16,8,1024]{2,1,0:T(8,128)}) fusion(f32[16,8,1024]{2,1,0:T(8,128)} %get-tuple-element.5, f32[16,8,1024]{2,1,0:T(8,128)S(1)} %copy-done, f32[16,8,1024]{2,1,0:T(8,128)} %get-tuple-element.4), kind=kLoop, calls=%fused_computation | loop fusion | flops 262144 | bytes 2621440 | tf_op jit(solution)/shard_map/sub | solution.py:626
Async XLA Ops:
  0.6 59.8 %copy-start = (f32[16,8,1024]{2,1,0:T(8,128)S(1)}, f32[16,8,1024]{2,1,0:T(8,128)}, u32[]{:S(2)}) copy-start(f32[16,8,1024]{2,1,0:T(8,128)} %c0_hbm.1) | copy-start | bytes 1572868
